TPU v7x, 32 devices: a whole 2x2x4 slice. The times are simulated.
32 devices in a mesh: expert: 2 (over x), dp: 16 (over z, y, core).
Axes of the slice: x: 2, y: 2, z: 4, core: 2. Of those that a mesh axis runs over, the one named last changes fastest.
Arguments:
- tokens_in: bfloat16 [2048, 7168], P('dp', 'expert'), may hold values from -6 to 6
- out_grad: bfloat16 [2048, 7168], P('dp', 'expert'), may hold values from -0.59765625 to 0.59765625
- expert_ids: int32 [2048, 8], P('dp'), may hold values from 0 to 15, all different within a row; in each aligned block of 128 rows (0 to 127, 128 to 255, ...) at most 80 rows name the same one
- route_weight: bfloat16 [2048, 8], P('dp'), may hold values from 0.019897461 to 0.5
- gate_weight: bfloat16 [16, 7168, 1024], P('dp', 'expert'), may hold values from -0.0625 to 0.0625
- up_weight: bfloat16 [16, 7168, 1024], P('dp', 'expert'), may hold values from -0.0625 to 0.0625
- down_weight: bfloat16 [16, 1024, 7168], P('dp', None, 'expert'), may hold values from -0.1875 to 0.1875
Outputs:
- input_grad: bfloat16 [2048, 7168], P('dp', 'expert')
- weight_grad: bfloat16 [2048, 8], P('dp')
- gate_grad: bfloat16 [16, 7168, 1024], P('dp', 'expert')
- up_grad: bfloat16 [16, 7168, 1024], P('dp', 'expert')
- down_grad: bfloat16 [16, 1024, 7168], P('dp', None, 'expert')
Inputs may be any that keep to these rules, and one draw needn't show every extreme that they name: `expert_ids`: each token names 8 different experts. Among the tokens of one dp index (aligned blocks of 128 tokens) no expert is named more than 80 times, a bound that some block reaches.
All inputs are finite; a program needn't handle non-finite values.
Results may differ from a plain program's by a relative error of at most 0.024.
Values may be sent and summed in bfloat16 or wider, within the bound.
No kernel may reach another device: no remote copies, remote signals or barrier semaphores. Data moves between devices by JAX's collectives and lax.ppermute only.
A program may use at most 192 MiB of HBM per device.

v0:
```python
import jax
import jax.numpy as jnp
from jax import lax
from jax.sharding import PartitionSpec as P


def swiglu_back(gate_sum, up_sum, back_sum, route_scale):
    gate_sigmoid = jax.nn.sigmoid(gate_sum)
    gate_silu = gate_sum * gate_sigmoid
    hidden = (gate_silu * up_sum).astype(jnp.bfloat16)
    dot_part = jnp.sum(hidden.astype(jnp.float32) * back_sum, axis=3)
    hidden_grad = route_scale[..., None] * back_sum
    grad_gate = (
        hidden_grad * up_sum * gate_sigmoid * (1.0 + gate_sum * (1.0 - gate_sigmoid))
    ).astype(jnp.bfloat16)
    grad_up = (hidden_grad * gate_silu).astype(jnp.bfloat16)
    return (hidden, dot_part, grad_gate, grad_up)


def body(tokens_in, out_grad, expert_ids, route_weight, gate_weight, up_weight, down_weight):
    token_count, top_count = expert_ids.shape
    experts_local = gate_weight.shape[0]
    width_local = tokens_in.shape[1]
    groups = lax.axis_size("dp")
    total_experts = experts_local * groups
    capacity = min(token_count, token_count * top_count * 5 // (4 * total_experts))
    routes = token_count * top_count
    flat_experts = expert_ids.reshape(-1)
    onehot = (flat_experts[:, None] == jnp.arange(total_experts, dtype=jnp.int32)[None, :]).astype(
        jnp.int32
    )
    route_rank = jnp.sum(onehot * (jnp.cumsum(onehot, axis=0) - 1), axis=1)
    slot_index = flat_experts * capacity + route_rank
    route_of_slot = (
        jnp.full((total_experts * capacity,), routes, jnp.int32)
        .at[slot_index]
        .set(jnp.arange(routes, dtype=jnp.int32))
    )
    filled = route_of_slot < routes
    safe_route = jnp.minimum(route_of_slot, routes - 1)
    token_of_slot = safe_route // top_count
    send_tokens = jnp.where(
        filled[:, None], tokens_in[token_of_slot], jnp.zeros((), tokens_in.dtype)
    )
    send_grads = jnp.where(filled[:, None], out_grad[token_of_slot], jnp.zeros((), out_grad.dtype))
    send_weights = jnp.where(
        filled, route_weight.reshape(-1)[safe_route], jnp.zeros((), route_weight.dtype)
    )
    recv_tokens, recv_grads, recv_weights = (
        lax.all_to_all(send_tokens, "dp", split_axis=0, concat_axis=0, tiled=True),
        lax.all_to_all(send_grads, "dp", split_axis=0, concat_axis=0, tiled=True),
        lax.all_to_all(send_weights, "dp", split_axis=0, concat_axis=0, tiled=True),
    )
    rows_in = recv_tokens.reshape(groups, experts_local, capacity, width_local)
    rows_back = recv_grads.reshape(groups, experts_local, capacity, width_local)
    route_scale = recv_weights.reshape(groups, experts_local, capacity).astype(jnp.float32)
    gate_part = jnp.einsum(
        "slcd,ldf->slcf", rows_in, gate_weight, preferred_element_type=jnp.float32
    )
    up_part = jnp.einsum("slcd,ldf->slcf", rows_in, up_weight, preferred_element_type=jnp.float32)
    back_part = jnp.einsum(
        "slcd,lfd->slcf", rows_back, down_weight, preferred_element_type=jnp.float32
    )
    gate_sum, up_sum, back_sum = (
        lax.psum_scatter(
            gate_part.astype(jnp.bfloat16), "expert", scatter_dimension=3, tiled=True
        ).astype(jnp.float32),
        lax.psum_scatter(
            up_part.astype(jnp.bfloat16), "expert", scatter_dimension=3, tiled=True
        ).astype(jnp.float32),
        lax.psum_scatter(
            back_part.astype(jnp.bfloat16), "expert", scatter_dimension=3, tiled=True
        ).astype(jnp.float32),
    )
    hidden, dot_part, grad_gate, grad_up = swiglu_back(gate_sum, up_sum, back_sum, route_scale)
    weight_dots = lax.psum(dot_part, "expert").astype(jnp.bfloat16)
    grad_gate, grad_up, hidden = (
        lax.all_gather(grad_gate, "expert", axis=3, tiled=True),
        lax.all_gather(grad_up, "expert", axis=3, tiled=True),
        lax.all_gather(hidden, "expert", axis=3, tiled=True),
    )
    gate_grad = jnp.einsum(
        "slcd,slcf->ldf", rows_in, grad_gate, preferred_element_type=jnp.float32
    ).astype(jnp.bfloat16)
    up_grad = jnp.einsum(
        "slcd,slcf->ldf", rows_in, grad_up, preferred_element_type=jnp.float32
    ).astype(jnp.bfloat16)
    scaled = (route_scale[..., None] * rows_back.astype(jnp.float32)).astype(jnp.bfloat16)
    down_grad = jnp.einsum(
        "slcf,slcd->lfd", hidden, scaled, preferred_element_type=jnp.float32
    ).astype(jnp.bfloat16)
    term_gate = jnp.einsum(
        "slcf,ldf->slcd", grad_gate, gate_weight, preferred_element_type=jnp.float32
    )
    term_up = jnp.einsum("slcf,ldf->slcd", grad_up, up_weight, preferred_element_type=jnp.float32)
    route_terms = (term_gate + term_up).astype(jnp.bfloat16)
    back_rows, back_weights = (
        lax.all_to_all(
            route_terms.reshape(-1, width_local), "dp", split_axis=0, concat_axis=0, tiled=True
        ),
        lax.all_to_all(weight_dots.reshape(-1), "dp", split_axis=0, concat_axis=0, tiled=True),
    )
    picked = back_rows[slot_index].reshape(token_count, top_count, width_local).astype(jnp.float32)
    input_grad = jnp.sum(picked, axis=1).astype(jnp.bfloat16)
    weight_grad = back_weights[slot_index].reshape(token_count, top_count)
    return (input_grad, weight_grad, gate_grad, up_grad, down_grad)


def solution(mesh):
    in_specs = (
        P("dp", "expert"),
        P("dp", "expert"),
        P("dp", None),
        P("dp", None),
        P("dp", "expert", None),
        P("dp", "expert", None),
        P("dp", None, "expert"),
    )
    out_specs = (
        P("dp", "expert"),
        P("dp", None),
        P("dp", "expert", None),
        P("dp", "expert", None),
        P("dp", None, "expert"),
    )
    return jax.shard_map(body, mesh=mesh, in_specs=in_specs, out_specs=out_specs, check_vma=False)
```

profile of v0, /device:TPU:13, one launch (start us, length us, event | category | flops | bytes accessed | tf_op | source)
XLA Modules:
  0.0 861.0 jit_solution(16285497697632105916)
XLA Ops:
  7.2 0.8 broadcast_multiply_fusion
  8.0 0.8 copy.29
  8.7 0.1 eq.29
  8.8 0.1 eq.25
  8.9 0.8 copy.33
  9.7 0.1 reshape.171
  9.8 0.1 copy.28
  9.9 0.1 mul.64
  10.0 4.5 reduce-window.6
  14.6 0.1 copy.31
  14.9 0.1 add_add_fusion
  15.1 4.3 scatter_custom_fusion
  19.4 8.0 gather_fusion
  27.4 0.1 broadcast_in_dim.39
  27.5 7.9 gather_fusion.2
  35.4 7.8 gather_fusion.1
  43.2 11.3 %broadcast_select_fusion.1 = (bf16[16,80,3584]{2,1,0:T(8,128)(2,1)}, bf16[16,80,3584]{2,1,0:T(8,128)(2,1)S(1)}) fusion(bf16[16,80,3584]{2,1,0:T(8,128)(2,1)} %bitcast.104, pred[16,80]{1,0:T(8,128)(4,1)S(1)} %broadcast_in_dim.39, bf16[16,80,3584]{2,1,0:T(8,128)(2,1)} %bitcast.103), kind=kLoop, calls=%fused_computation.14 | loop fusion | flops 9175040 | bytes 36701440 | tf_op jit(solution)/shard_map/jit(_where)/select_n | solution.py:45
  54.5 205.4 %all_to_all.43 = bf16[16,80,3584]{2,1,0:T(8,128)(2,1)} all-to-all(bf16[16,80,3584]{2,1,0:T(8,128)(2,1)S(1)} %get-tuple-element.29), channel_id=1, replica_groups=mesh['expert'=2,'dp'=16] {'dp'}, dimensions={0} | all-to-all | bytes 18350080 | tf_op jit(solution)/shard_map/all_to_all | solution.py:50
  260.0 5.8 all-to-all-start.1
  265.8 15.3 %convert_bitcast_fusion = bf16[16,1,80,1024]{3,2,0,1:T(8,128)(2,1)} fusion(bf16[16,80,3584]{2,1,0:T(8,128)(2,1)} %all_to_all.43, bf16[1,3584,1024]{2,1,0:T(8,128)(2,1)} %param.11), kind=kOutput, calls=%fused_computation.51 | convolution fusion | flops 9396551680 | bytes 19136512 | tf_op jit(solution)/shard_map/slcd,ldf->slcf/dot_general | solution.py:57
  281.2 15.3 %convert_bitcast_fusion.1 = bf16[16,1,80,1024]{3,2,0,1:T(8,128)(2,1)} fusion(bf16[16,80,3584]{2,1,0:T(8,128)(2,1)} %all_to_all.43, bf16[1,3584,1024]{2,1,0:T(8,128)(2,1)} %param.12), kind=kOutput, calls=%fused_computation.52 | convolution fusion | flops 9396551680 | bytes 19136512 | tf_op jit(solution)/shard_map/slcd,ldf->slcf/dot_general | solution.py:60
  296.6 0.3 reduce-scatter.4.cloned.1.call-start
  296.9 168.1 %all-to-all-done.1 = bf16[16,80,3584]{2,1,0:T(8,128)(2,1)} async-done(((bf16[16,80,3584]{2,1,0:T(8,128)(2,1)}), bf16[16,80,3584]{2,1,0:T(8,128)(2,1)}, u32[]{:S(2)}, u32[]{:S(2)}) %all-to-all-start.1) | async-done | bytes 9175072 | tf_op jit(solution)/shard_map/all_to_all | solution.py:51
  465.0 15.4 %convert_bitcast_fusion.2 = bf16[16,1,80,1024]{3,2,0,1:T(8,128)(2,1)} fusion(bf16[16,80,3584]{2,1,0:T(8,128)(2,1)} %all-to-all-done.1, bf16[1,1024,3584]{2,1,0:T(8,128)(2,1)} %param.13), kind=kOutput, calls=%fused_computation.53 | convolution fusion | flops 9396551680 | bytes 19136512 | tf_op jit(solution)/shard_map/slcd,lfd->slcf/dot_general | solution.py:61
  480.5 8.5 all_to_all.44
  489.1 28.5 %reduce-scatter.4.cloned.1.call-done = bf16[16,1,80,512]{3,2,0,1:T(8,128)(2,1)} async-done(((bf16[16,1,80,1024]{3,2,0,1:T(8,128)(2,1)}), bf16[16,1,80,512]{3,2,0,1:T(8,128)(2,1)}) %reduce-scatter.4.cloned.1.call-update) | async-done | bytes 1310736 | tf_op jit(solution)/shard_map/reduce_scatter | solution.py:71
  517.6 4.9 fusion.16
  522.5 3.9 psum.7
  526.4 0.6 copy.35
  527.0 7.5 all-to-all-start.4
  534.6 0.5 all-gather.6.cloned.1.call-update
  535.1 26.6 %all-gather.4.cloned.1.call-done = bf16[16,1,80,1024]{3,2,0,1:T(8,128)(2,1)} async-done(((bf16[16,1,80,512]{3,2,0,1:T(8,128)(2,1)}), bf16[16,1,80,1024]{3,2,0,1:T(8,128)(2,1)}) %all-gather.4.cloned.1.call-update) | async-done | bytes 2621456 | tf_op jit(solution)/shard_map/all_gather | solution.py:78
  561.7 16.4 %fusion.2 = f32[16,80,3584]{2,1,0:T(8,128)} fusion(bf16[1,3584,1024]{2,1,0:T(8,128)(2,1)} %param.11, bf16[16,1,80,1024]{3,2,0,1:T(8,128)(2,1)} %all-gather.4.cloned.1.call-done), kind=kOutput, calls=%fused_computation.16 | convolution fusion | flops 9395240960 | bytes 28311552 | tf_op jit(solution)/shard_map/slcf,ldf->slcd/dot_general | solution.py:92
  578.2 24.7 %all-gather.6.cloned.1.call-done = bf16[16,1,80,1024]{3,2,0,1:T(8,128)(2,1)} async-done(((bf16[16,1,80,512]{3,2,0,1:T(8,128)(2,1)}), bf16[16,1,80,1024]{3,2,0,1:T(8,128)(2,1)}) %all-gather.6.cloned.1.call-update) | async-done | bytes 2621456 | tf_op jit(solution)/shard_map/all_gather | solution.py:79
  602.8 17.6 %add_convert_fusion = bf16[16,80,3584]{2,1,0:T(8,128)(2,1)} fusion(f32[16,80,3584]{2,1,0:T(8,128)} %fusion.2, bf16[1,3584,1024]{2,1,0:T(8,128)(2,1)} %param.12, bf16[16,1,80,1024]{3,2,0,1:T(8,128)(2,1)} %all-gather.6.cloned.1.call-done), kind=kOutput, calls=%fused_computation.7 | convolution fusion | flops 9404416000 | bytes 37486592 | tf_op jit(solution)/shard_map/slcf,ldf->slcd/dot_general | solution.py:95
  620.5 6.4 all-to-all-start.3
  626.9 0.5 all-gather.8.cloned.1.call-update
  627.5 0.1 all_to_all.36
  627.6 15.5 %gather_fusion.4 = bf16[1024]{0:T(1024)(128)(2,1)S(1)} fusion(bf16[1280]{0:T(1024)(128)(2,1)S(1)} %all_to_all.36, s32[1024]{0:T(1024)S(1)} %broadcast_clamp_fusion), kind=kCustom, calls=%fused_computation.4 | custom fusion | bytes 8192 | tf_op jit(solution)/shard_map/gather | solution.py:105
  643.1 0.1 reshape.178
  643.2 0.7 copy.36
  643.8 24.4 %all-gather.8.cloned.1.call-done = bf16[16,1,80,1024]{3,2,0,1:T(8,128)(2,1)} async-done(((bf16[16,1,80,512]{3,2,0,1:T(8,128)(2,1)}), bf16[16,1,80,1024]{3,2,0,1:T(8,128)(2,1)}) %all-gather.8.cloned.1.call-update) | async-done | bytes 2621456 | tf_op jit(solution)/shard_map/all_gather | solution.py:80
  668.3 15.7 %fusion.13 = bf16[1,1024,3584]{2,1,0:T(8,128)(2,1)} fusion(bf16[16,80,3584]{2,1,0:T(8,128)(2,1)} %all-to-all-done.1, f32[16,80]{1,0:T(8,128)S(1)} %bitcast.109, bf16[16,1,80,1024]{3,2,0,1:T(8,128)(2,1)} %all-gather.8.cloned.1.call-done), kind=kOutput, calls=%fused_computation.27 | convolution fusion | flops 9412673536 | bytes 19141632 | tf_op jit(solution)/shard_map/slcf,slcd->lfd/dot_general | solution.py:89
  684.0 15.4 %fusion.12 = bf16[1,3584,1024]{2,1,0:T(8,128)(2,1)} fusion(bf16[16,80,3584]{2,1,0:T(8,128)(2,1)} %all_to_all.43, bf16[16,1,80,1024]{3,2,0,1:T(8,128)(2,1)S(1)} %copy-done.6), kind=kOutput, calls=%fused_computation.26 | convolution fusion | flops 9398910976 | bytes 19136512 | tf_op jit(solution)/shard_map/slcd,slcf->ldf/dot_general | solution.py:85
  699.4 11.8 %fusion.11 = bf16[1,3584,1024]{2,1,0:T(8,128)(2,1)} fusion(bf16[16,80,3584]{2,1,0:T(8,128)(2,1)S(1)} %bitcast.106, bf16[16,1,80,1024]{3,2,0,1:T(8,128)(2,1)S(1)} %copy-done.5), kind=kOutput, calls=%fused_computation.25 | convolution fusion | flops 9398910976 | bytes 19136512 | tf_op jit(solution)/shard_map/slcd,slcf->ldf/dot_general | solution.py:82
  711.2 114.8 %all-to-all-done.3 = bf16[16,80,3584]{2,1,0:T(8,128)(2,1)} async-done(((bf16[16,80,3584]{2,1,0:T(8,128)(2,1)}), bf16[16,80,3584]{2,1,0:T(8,128)(2,1)}, u32[]{:S(2)}, u32[]{:S(2)}) %all-to-all-start.3) | async-done | bytes 9175072 | tf_op jit(solution)/shard_map/all_to_all | solution.py:98
  826.1 18.9 %gather_fusion.3 = bf16[1024,3584]{1,0:T(8,128)(2,1)} fusion(bf16[1280,3584]{1,0:T(8,128)(2,1)} %bitcast.24, s32[1024]{0:T(1024)S(1)} %broadcast_clamp_fusion), kind=kCustom, calls=%fused_computation.3 | custom fusion | bytes 14684160 | tf_op jit(solution)/shard_map/gather | solution.py:103
  844.9 8.9 %bitcast_reduce_fusion = bf16[128,3584]{1,0:T(8,128)(2,1)} fusion(bf16[1024,3584]{1,0:T(8,128)(2,1)} %gather_fusion.3), kind=kLoop, calls=%fused_computation.15 | loop fusion | flops 3211264 | bytes 8257536 | tf_op jit(solution)/shard_map/reduce_sum | solution.py:104
  (48 shorter events, 0.7 us)
Async XLA Ops:
  7.2 20.3 %copy-start = (bf16[128,3584]{1,0:T(8,128)(2,1)S(1)}, bf16[128,3584]{1,0:T(8,128)(2,1)}, u32[]{:S(2)}) copy-start(bf16[128,3584]{1,0:T(8,128)(2,1)} %param.7) | copy-start | bytes 2752516
  15.0 4.4 copy-start.3
  27.5 7.9 copy-start.2
  260.0 205.0 %all-to-all-start.1 = ((bf16[16,80,3584]{2,1,0:T(8,128)(2,1)}), bf16[16,80,3584]{2,1,0:T(8,128)(2,1)}, u32[]{:S(2)}, u32[]{:S(2)}) async-start(bf16[16,80,3584]{2,1,0:T(8,128)(2,1)} %get-tuple-element.28), calls=%async_computation.1 | async-start | bytes 18350080 | tf_op jit(solution)/shard_map/all_to_all | solution.py:51
  265.8 223.3 %reduce-scatter.8.cloned.1.call-start = ((), (), s32[]{:S(2)}) async-start(), calls=%async_computation.10 | async-start | bytes 3932160 | tf_op jit(solution)/shard_map/reduce_scatter | solution.py:65
  281.2 207.9 %reduce-scatter.6.cloned.1.call-start = ((), (), s32[]{:S(2)}) async-start(), calls=%async_computation.9 | async-start | bytes 3932160 | tf_op jit(solution)/shard_map/reduce_scatter | solution.py:68
  296.6 221.0 %reduce-scatter.4.cloned.1.call-start = ((), (), s32[]{:S(2)}) async-start(), calls=%async_computation.8 | async-start | bytes 3932160 | tf_op jit(solution)/shard_map/reduce_scatter | solution.py:71
  480.4 81.3 %all-gather.4.cloned.1.call-start = ((), (), s32[]{:S(2)}) async-start(), calls=%async_computation.11 | async-start | bytes 3932160 | tf_op jit(solution)/shard_map/all_gather | solution.py:78
  527.0 93.5 %all-to-all-start.4 = ((bf16[16,80,1]{1,2,0:T(2,128)(2,1)}), bf16[16,80,1]{1,2,0:T(2,128)(2,1)S(1)}, u32[]{:S(2)}, u32[]{:S(2)}) async-start(bf16[16,80,1]{1,2,0:T(2,128)(2,1)} %copy.35), calls=%async_computation.7 | async-start | bytes 16384 | tf_op jit(solution)/shard_map/all_to_all | solution.py:101
  534.5 68.3 %all-gather.6.cloned.1.call-start = ((), (), s32[]{:S(2)}) async-start(), calls=%async_computation.12 | async-start | bytes 3932160 | tf_op jit(solution)/shard_map/all_gather | solution.py:79
  620.5 7.0 copy-start.4
  620.5 205.6 %all-to-all-start.3 = ((bf16[16,80,3584]{2,1,0:T(8,128)(2,1)}), bf16[16,80,3584]{2,1,0:T(8,128)(2,1)}, u32[]{:S(2)}, u32[]{:S(2)}) async-start(bf16[16,80,3584]{2,1,0:T(8,128)(2,1)} %add_convert_fusion), calls=%async_computation.6 | async-start | bytes 18350080 | tf_op jit(solution)/shard_map/all_to_all | solution.py:98
  626.9 41.4 %all-gather.8.cloned.1.call-start = ((), (), s32[]{:S(2)}) async-start(), calls=%async_computation.13 | async-start | bytes 3932160 | tf_op jit(solution)/shard_map/all_gather | solution.py:80
  643.8 40.1 %copy-start.6 = (bf16[16,1,80,1024]{3,2,0,1:T(8,128)(2,1)S(1)}, bf16[16,1,80,1024]{3,2,0,1:T(8,128)(2,1)}, u32[]{:S(2)}) copy-start(bf16[16,1,80,1024]{3,2,0,1:T(8,128)(2,1)} %all-gather.6.cloned.1.call-done) | copy-start | bytes 7864324
  668.3 31.1 %slice-start = ((s8[9175040]{0:T(1024)(128)(4,1)}), s8[786432]{0:T(1024)(128)(4,1)S(1)}, s32[]{:S(2)}) async-start(s8[9175040]{0:T(1024)(128)(4,1)} %bitcast.105), calls=%async_computation.14 | async-start | bytes 1572864
  668.3 31.1 %slice-start.1 = ((s8[9175040]{0:T(1024)(128)(4,1)}), s8[4194304]{0:T(1024)(128)(4,1)S(1)}, s32[]{:S(2)}) async-start(s8[9175040]{0:T(1024)(128)(4,1)} %bitcast.105), calls=%async_computation.15 | async-start | bytes 8388608
  684.0 15.4 %slice-start.2 = ((s8[9175040]{0:T(1024)(128)(4,1)}), s8[4194304]{0:T(1024)(128)(4,1)S(1)}, s32[]{:S(2)}) async-start(s8[9175040]{0:T(1024)(128)(4,1)} %bitcast.105), calls=%async_computation.16 | async-start | bytes 8388608
  684.0 15.4 %copy-start.5 = (bf16[16,1,80,1024]{3,2,0,1:T(8,128)(2,1)S(1)}, bf16[16,1,80,1024]{3,2,0,1:T(8,128)(2,1)}, u32[]{:S(2)}) copy-start(bf16[16,1,80,1024]{3,2,0,1:T(8,128)(2,1)} %all-gather.4.cloned.1.call-done) | copy-start | bytes 7864324
  826.1 27.8 %copy-start.1 = (bf16[128,3584]{1,0:T(8,128)(2,1)S(1)}, bf16[128,3584]{1,0:T(8,128)(2,1)}, u32[]{:S(2)}) copy-start(bf16[128,3584]{1,0:T(8,128)(2,1)} %param.7) | copy-start | bytes 2752516
Sparse Core Ops, SparseCore 0:
  281.3 38.1 reduce-scatter.7
  322.4 37.5 reduce-scatter.5
  480.5 37.0 reduce-scatter.3
  522.7 39.0 all-gather.3
  563.8 39.0 all-gather.5
  629.6 38.6 all-gather.7
where the time goes:
time: 870 us; the launch traced here: 861 us
  waiting for transfers between devices  388 us (45%)
  blocking collectives  218 us (25%)
  matrix products  123 us (14%)
  local copies, waits for them, and re-layouts  66.4 us (8%)
  other arithmetic  30.7 us (4%)
  starting transfers between devices  20.2 us (2%)
  between operations  14.5 us (2%)
    all_to_all x1, blocking collectives, body(): lax.all_to_all(send_tokens, 'dp', split_axis=0, concat_axis=0, tiled=True)  205 us
    all_to_all x1, waiting for transfers between devices, body(): lax.all_to_all(send_grads, 'dp', split_axis=0, concat_axis=0, tiled=True)  168 us
    all_to_all x1, waiting for transfers between devices, body(): lax.all_to_all(route_terms.reshape(-1, width_local), 'dp', split_axis=0,...  115 us
    reduce_scatter x1, waiting for transfers between devices, body(): lax.psum_scatter(back_part.astype(jnp.bfloat16), 'expert', scatter_dimens...  28.5 us
    all_gather x1, waiting for transfers between devices, body(): lax.all_gather(grad_gate, 'expert', axis=3, tiled=True)  26.6 us
    all_gather x1, waiting for transfers between devices, body(): lax.all_gather(grad_up, 'expert', axis=3, tiled=True)  24.7 us
    all_gather x1, waiting for transfers between devices, body(): lax.all_gather(hidden, 'expert', axis=3, tiled=True)  24.4 us
    gather x1, local copies, waits for them, and re-layouts, body(): back_rows[slot_index].reshape(token_count, top_count, width_local)  18.9 us
  transfers between devices with their start and end apart: 9, of which 6 were waited for; matrix products, arithmetic and copies ran while one was open for 16% of the time, Pallas kernels for 0%

commit v1 on v0

v1 whole, which is shorter than its diff:
```python
import functools

import jax
import jax.numpy as jnp
from jax import lax
from jax.experimental import pallas as pl
from jax.experimental.pallas import tpu as pltpu
from jax.sharding import PartitionSpec as P

BF16 = jnp.bfloat16
F32 = jnp.float32
LANES = 128
VMEM_LIMIT = 44 * 1024 * 1024


def split_dp(size):
    core = 2 if size % 2 == 0 else 1
    chips = size // core
    inner = 1
    while chips % (inner * 2) == 0 and (inner * 2) * (inner * 2) <= chips:
        inner *= 2
    return chips // inner, inner, core


def tile_of(size, most):
    best = LANES
    for tile in range(LANES, most + 1, LANES):
        if size % tile == 0:
            best = tile
    return best


def dot(a, b, dims=((1,), (0,))):
    return lax.dot_general(a, b, (dims, ((), ())), preferred_element_type=F32)


def cost(flops, moved):
    return pl.CostEstimate(flops=flops, bytes_accessed=moved, transcendentals=0)


def gate(x, after):
    return x if after is None or (isinstance(after, tuple) and not after) else lax.optimization_barrier((x, after))[0]


def whole(shape):
    zeros = (0,) * len(shape)
    return pl.BlockSpec(shape, lambda *_: zeros)


def choose(pick_t, block_ref, cols, slots):
    pick = jnp.transpose(pick_t.astype(F32))[:slots].astype(BF16)
    return dot(pick, block_ref[:, cols]).astype(BF16)


def fore_kernel(n, slots, top, width, step_cols, *refs):
    me_ref, block_refs = refs[0], refs[1 : 1 + n]
    gate_ref, up_ref = refs[1 + n : 3 + n]
    rows_ref, part_ref, pick_ref, scale_ref = refs[-4:]

    @pl.when(pl.program_id(0) == 0)
    def _():
        me = me_ref[0].astype(F32)
        count = block_refs[0].shape[0]
        lower = (
            lax.broadcasted_iota(jnp.int32, (count, count), 1)
            < lax.broadcasted_iota(jnp.int32, (count, count), 0)
        ).astype(BF16)
        lane = lax.broadcasted_iota(jnp.int32, (count, LANES), 1).astype(F32)
        for b in range(n):
            meta = block_refs[b][:, width : width + LANES].astype(F32)
            hit = (meta[:, :top] == me).astype(F32)
            chosen = jnp.max(hit, axis=1, keepdims=True)
            weight = jnp.sum(hit * meta[:, top : 2 * top], axis=1, keepdims=True)
            chosen = jnp.broadcast_to(chosen, (count, LANES))
            order = dot(lower, chosen.astype(BF16))
            pick_t = jnp.where((order == lane) & (chosen > 0.5), 1.0, 0.0)
            pick_ref[b] = pick_t.astype(BF16)
            pick = jnp.transpose(pick_t)[:slots].astype(BF16)
            at = pl.ds(b * slots, slots)
            scale_ref[at, :] = dot(pick, jnp.broadcast_to(weight, (count, LANES)).astype(BF16))
            for left in range(0, width, step_cols):
                cols = slice(left, left + step_cols)
                rows_ref[at, cols] = dot(pick, block_refs[b][:, cols]).astype(BF16)

    rows = rows_ref[...]
    part_ref[0] = dot(rows, gate_ref[0]).astype(BF16)
    part_ref[1] = dot(rows, up_ref[0]).astype(BF16)


def back_kernel(n, slots, width, step_cols, *refs):
    block_refs = refs[1 : 1 + n]
    pick_ref, scale_ref, down_ref = refs[1 + n : n + 4]
    scaled_ref, part_ref, rows_ref = refs[-3:]

    @pl.when(pl.program_id(0) == 0)
    def _():
        for b in range(n):
            pick = jnp.transpose(pick_ref[b].astype(F32))[:slots].astype(BF16)
            at = pl.ds(b * slots, slots)
            scale = scale_ref[at, :1]
            for left in range(0, width, step_cols):
                cols = slice(left, left + step_cols)
                picked = dot(pick, block_refs[b][0, :, cols])
                rows_ref[at, cols] = picked.astype(BF16)
                scaled_ref[at, cols] = (scale * picked).astype(BF16)

    part_ref[...] = dot(rows_ref[...], down_ref[0], ((1,), (1,))).astype(BF16)


def act_kernel(n_in, n_core, slots, units, width, tile, n_parts, *refs):
    me_ref = refs[0]
    fore_refs, back_refs = refs[1 : 1 + n_parts], refs[1 + n_parts : 1 + 2 * n_parts]
    pick_ref, scale_ref, gate_ref, up_ref = refs[1 + 2 * n_parts : 5 + 2 * n_parts]
    hidden_ref, dgate_ref, dup_ref = refs[-3 - n_core : -n_core]
    dense_refs = refs[-n_core:]
    step = pl.program_id(0)

    def scatter(b, values):
        pick_t = pick_ref[b][:, :slots]
        return dot(pick_t, values).astype(BF16)

    @pl.when(step == 0)
    def _():
        for b in range(n_in * n_core):
            at = pl.ds(b * slots, slots)
            total = jnp.zeros((slots, 1), F32)
            scale = scale_ref[at, :1]
            cut = tile_of(units, 256)
            for left in range(0, units, cut):
                cols = slice(left, left + cut)
                gate_sum = sum(f[0, at, cols].astype(F32) for f in fore_refs)
                up_sum = sum(f[1, at, cols].astype(F32) for f in fore_refs)
                back_sum = sum(f[at, cols].astype(F32) for f in back_refs)
                sig = jax.nn.sigmoid(gate_sum)
                silu = gate_sum * sig
                hidden = (silu * up_sum).astype(BF16)
                hidden_ref[at, cols] = hidden
                total = total + jnp.sum(hidden.astype(F32) * back_sum, axis=1, keepdims=True)
                q = scale * back_sum
                dgate_ref[at, cols] = (q * up_sum * sig * (1.0 + gate_sum * (1.0 - sig))).astype(BF16)
                dup_ref[at, cols] = (q * silu).astype(BF16)
            extra = dense_refs[0].shape[2] - width
            lane = lax.broadcasted_iota(jnp.int32, (slots, extra), 1)
            held = jnp.where(lane == me_ref[0], total, 0.0).astype(BF16)
            dense_refs[b % n_core][b // n_core, :, width:] = scatter(b, held)

    term = dot(dgate_ref[...], gate_ref[0], ((1,), (1,))) + dot(
        dup_ref[...], up_ref[0], ((1,), (1,))
    )
    term = term.astype(BF16)
    cols = pl.ds(pl.multiple_of(step * tile, LANES), tile)
    for b in range(n_in * n_core):
        dense_refs[b % n_core][b // n_core, :, cols] = scatter(
            b, term[b * slots : (b + 1) * slots]
        )


def body(tokens_in, out_grad, expert_ids, route_weight, gate_weight, up_weight, down_weight):
    token_count, top_count = expert_ids.shape
    experts_local, width, units = gate_weight.shape
    groups = lax.axis_size("dp")
    n_expert = lax.axis_size("expert")
    total_experts = experts_local * groups
    capacity = min(token_count, token_count * top_count * 5 // (4 * total_experts))
    slots = -(-capacity // 16) * 16
    n_out, n_in, n_core = split_dp(groups)
    me = lax.axis_index("dp")
    me_arr = me.astype(jnp.int32).reshape(1)
    sizes = (n_out, n_in, n_core)
    members = n_in * n_core
    rows = members * slots
    extra = LANES * (-(-total_experts // LANES))
    step_cols = tile_of(width, 512)

    def shift(x, axis, step, name):
        pairs = []
        for o in range(n_out):
            for i in range(n_in):
                for c in range(n_core):
                    at = [o, i, c]
                    dst = (o * n_in + i) * n_core + c
                    at[axis] = (at[axis] + step) % sizes[axis]
                    src = (at[0] * n_in + at[1]) * n_core + at[2]
                    pairs.append((src, dst))
        with jax.named_scope(name):
            return lax.ppermute(x, "dp", pairs)

    def source(r, i, c):
        at = (me // (n_in * n_core) + r) % n_out, (me // n_core + i) % n_in, (me + c) % n_core
        return ((at[0] * n_in + at[1]) * n_core + at[2]).astype(jnp.int32)

    near = sorted(range(n_out), key=lambda r: (min(r, n_out - r), r))
    far = near[::-1]

    def exchange(part, name):
        parts = [part]
        for step in range(1, n_expert):
            pairs = [((k + step) % n_expert, k) for k in range(n_expert)]
            with jax.named_scope(name + "_x"):
                parts.append(lax.ppermute(part, "expert", pairs))
        return parts

    smem = pl.BlockSpec(memory_space=pltpu.SMEM)
    anywhere = pl.BlockSpec(memory_space=pl.ANY)

    def at_rows(r, cols):
        return pl.BlockSpec((rows, cols), lambda j: (r, 0))

    def call(kernel, name, grid, ins, in_specs, outs, out_specs, before, flops, scratch=()):
        aliases = {}
        if before is not None:
            for k, held in enumerate(before):
                aliases[len(ins)] = k
                ins = [*ins, held]
                in_specs = [*in_specs, anywhere]
        return pl.pallas_call(
            kernel,
            grid=(grid,),
            in_specs=in_specs,
            out_specs=out_specs,
            out_shape=outs,
            scratch_shapes=scratch,
            input_output_aliases=aliases,
            compiler_params=pltpu.CompilerParams(vmem_limit_bytes=VMEM_LIMIT),
            cost_estimate=cost(flops // 1000, 0),
            name=name,
        )(*ins)

    def sds(shape, dtype=BF16):
        return jax.ShapeDtypeStruct(shape, dtype)

    unit_tile = tile_of(units, 256)
    all_rows = n_out * rows

    def fore_call(r, blocks, before):
        def kernel(*refs):
            fore_kernel(members, slots, top_count, width, step_cols, *refs[: 3 + members], *refs[-4:])

        weight = pl.BlockSpec((1, width, unit_tile), lambda j: (0, 0, j))
        return call(
            kernel,
            f"fore{r}",
            units // unit_tile,
            [me_arr, *blocks, gate_weight, up_weight],
            [smem, *[whole(b.shape) for b in blocks], weight, weight],
            [
                sds((all_rows, width)),
                sds((2, rows, units)),
                sds((members, token_count, LANES)),
                sds((rows, LANES), F32),
            ],
            [
                at_rows(r, width),
                pl.BlockSpec((2, rows, unit_tile), lambda j: (0, 0, j)),
                whole((members, token_count, LANES)),
                whole((rows, LANES)),
            ],
            before,
            2 * rows * width * 2 * units,
        )

    def back_call(r, grads, pick, scale, before):
        def kernel(*refs):
            back_kernel(members, slots, width, step_cols, *refs[: 4 + members], *refs[-3:])

        places = jnp.stack([source(r, i, c) for i in range(n_in) for c in range(n_core)])
        ins = [places, *[grads] * members, pick, scale, down_weight]
        in_specs = [
            pl.BlockSpec((1, token_count, width), lambda j, at, b=b: (at[b], 0, 0))
            for b in range(members)
        ]
        in_specs += [
            whole(pick.shape),
            whole(scale.shape),
            pl.BlockSpec((1, unit_tile, width), lambda j, at: (0, j, 0)),
        ]
        aliases = {}
        if before is not None:
            aliases[len(ins)] = 0
            ins.append(before[0])
            in_specs.append(anywhere)
        return pl.pallas_call(
            kernel,
            grid_spec=pltpu.PrefetchScalarGridSpec(
                num_scalar_prefetch=1,
                grid=(units // unit_tile,),
                in_specs=in_specs,
                out_specs=[
                    pl.BlockSpec((rows, width), lambda j, at: (r, 0)),
                    pl.BlockSpec((rows, unit_tile), lambda j, at: (0, j)),
                ],
                scratch_shapes=[pltpu.VMEM((rows, width), BF16)],
            ),
            out_shape=[sds((all_rows, width)), sds((rows, units))],
            input_output_aliases=aliases,
            compiler_params=pltpu.CompilerParams(vmem_limit_bytes=VMEM_LIMIT),
            cost_estimate=cost(2 * rows * width * units // 1000, 0),
            name=f"back{r}",
        )(*ins)

    def act_call(r, fore, back, pick, scale, before):
        tile = step_cols

        def kernel(*refs):
            act_kernel(
                n_in, n_core, slots, units, width, tile, n_expert,
                *refs[: 5 + 2 * n_expert], *refs[-3 - n_core :],
            )

        weight = pl.BlockSpec((1, tile, units), lambda j: (0, j, 0))
        dense = (n_in, token_count, width + extra)
        return call(
            kernel,
            f"act{r}",
            width // tile,
            [me_arr, *fore, *back, pick, scale, gate_weight, up_weight],
            [
                smem,
                *[whole(x.shape) for x in (*fore, *back, pick, scale)],
                weight,
                weight,
            ],
            [*[sds((all_rows, units))] * 3, *[sds(dense)] * n_core],
            [*[at_rows(r, units)] * 3, *[whole(dense)] * n_core],
            before,
            2 * rows * width * 2 * units,
        )

    meta = jnp.concatenate([expert_ids.astype(BF16), route_weight], axis=1)
    meta = jnp.pad(meta, ((0, 0), (0, LANES - meta.shape[1])))
    tokens = jnp.concatenate([tokens_in, meta], axis=1)

    rest = near[1:]
    turn = rest[::-1] + [0]
    fore, back, pick, scale, sums, lines_of = {}, {}, {}, {}, {}, {}
    hold = {"fore": None, "back": None, "act": None}
    y_done = []

    def done(kind):
        return hold[kind][0]

    def run_lines(r, block, after):
        lines = [block]
        for i in range(1, n_in):
            x = gate(block, (*after, *y_done[-1:]))
            y_done.append(shift(x, 1, i, f"tok{r}_y"))
            lines.append(y_done[-1])
        return lines

    def run_fore(r, lines, *after):
        blocks = []
        for line in lines:
            blocks.append(line)
            for c in range(1, n_core):
                blocks.append(shift(line, 2, c, f"tok{r}_core"))
        blocks[0] = gate(blocks[0], after)
        rows_in, part, pick[r], scale[r] = fore_call(r, blocks, hold["fore"])
        hold["fore"] = [rows_in]
        fore[r] = exchange(part, f"fore{r}")

    def run_back(r, *after):
        rows_back, part = back_call(r, gate(grads, after), pick[r], scale[r], hold["back"])
        hold["back"] = [rows_back]
        back[r] = exchange(part, f"back{r}")

    def run_act(r, *after):
        came = [gate(back[r][0], after), *back[r][1:]]
        hidden, dgate, dup, *dense = act_call(r, fore[r], came, pick[r], scale[r], hold["act"])
        hold["act"] = [hidden, dgate, dup]
        came = [shift(dense[c], 2, -c, f"sum{r}_core") for c in range(1, n_core)]
        lines_of[r] = [
            sum([x[i].astype(F32) for x in came], dense[0][i].astype(F32)).astype(BF16)
            for i in range(n_in)
        ]

    def run_sum(r, acted, came, before):
        after = tuple(x for x in (came, before) if x is not None)
        total = gate(lines_of[r][0], acted).astype(F32)
        for i in range(1, n_in):
            total = total + shift(gate(lines_of[r][i], after), 1, -i, f"sum{r}_y").astype(F32)
        sums[r] = total = total.astype(BF16)
        if r:
            sums[r] = shift(total, 0, -r, f"sum{r}_z")
        return total

    block = {0: tokens}
    for k, r in enumerate(rest):
        block[r] = shift(gate(tokens, block[rest[k - 2]] if k >= 2 else None), 0, r, f"tok{r}_z")
    grads = lax.all_gather(gate(out_grad, None), "dp", axis=0)
    lines = {0: run_lines(0, tokens, ())}
    for k, r in enumerate(near):
        if k + 1 < n_out:
            lines[near[k + 1]] = run_lines(near[k + 1], block[near[k + 1]], ())
        run_fore(r, lines[r])
        before = (done("fore"), *([fore[near[k - 1]][-1]] if k else []))
        if k + 1 < n_out:
            nxt = near[k + 1]
            lines[nxt] = [gate(line, before) for line in lines[nxt]]
        if k + 2 < n_out:
            nxt = near[k + 2]
            block[nxt] = gate(block[nxt], done("fore"))
    for k, r in enumerate(turn):
        run_back(r, done("fore"), *([fore[near[-1]][-1]] if k else [fore[near[-2]][-1]]))
    total = None
    for k, r in enumerate(turn):
        run_act(r, done("back"), *([] if k == 0 else [lines_of[turn[k - 1]][-1]]))
        if k:
            total = run_sum(turn[k - 1], done("act"), back[r][-1], total)
    run_sum(turn[-1], None, None, total)
    rows_in, rows_back = hold["fore"][0], hold["back"][0]
    hidden, dgate, dup = hold["act"]
    full = sum(sums[r].astype(F32) for r in near)
    input_grad = full[:, :width].astype(BF16)
    dots_of = full[:, width : width + total_experts]
    named = expert_ids[:, :, None] == jnp.arange(total_experts, dtype=jnp.int32)[None, None, :]
    weight_grad = jnp.sum(jnp.where(named, dots_of[:, None, :], 0.0), axis=2).astype(BF16)

    gate_grad = dot(rows_in, dgate, ((0,), (0,))).astype(BF16)
    up_grad = dot(rows_in, dup, ((0,), (0,))).astype(BF16)
    down_grad = dot(hidden, rows_back, ((0,), (0,))).astype(BF16)
    return (input_grad, weight_grad, gate_grad[None], up_grad[None], down_grad[None])


def solution(mesh):
    in_specs = (
        P("dp", "expert"),
        P("dp", "expert"),
        P("dp", None),
        P("dp", None),
        P("dp", "expert", None),
        P("dp", "expert", None),
        P("dp", None, "expert"),
    )
    out_specs = (
        P("dp", "expert"),
        P("dp", None),
        P("dp", "expert", None),
        P("dp", "expert", None),
        P("dp", None, "expert"),
    )
    return jax.shard_map(body, mesh=mesh, in_specs=in_specs, out_specs=out_specs, check_vma=False)
```

time: 870 us -> 464 us (0.53)
  blocking collectives: 218 us -> 0 us
  waiting for transfers between devices: 388 us -> 194 us
  Pallas kernels: 0 us -> 129 us
  matrix products: 123 us -> 37.4 us
  local copies, waits for them, and re-layouts: 66.4 us -> 12 us
  starting transfers between devices: 20.2 us -> 60.7 us
  other arithmetic: 30.7 us -> 12.4 us
    all_to_all x3 -> x0, waiting for transfers between devices: 283 us -> none  [the longest x1 168 us: body(): lax.all_to_all(send_grads, 'dp', split_axis=0, concat_axis=0, tiled=True)]
    all_to_all x2 -> x0, blocking collectives: 214 us -> none  [the longest x1 205 us: body(): lax.all_to_all(send_tokens, 'dp', split_axis=0, concat_axis=0, tiled=True)]
    ppermute x0 -> x34, waiting for transfers between devices: none -> 194 us  [the longest x26 138 us: shift(): return lax.ppermute(x, 'dp', pairs)]
    pallas_call x0 -> x12, Pallas kernels: none -> 129 us  [the longest x8 97 us: call(): pl.pallas_call(kernel, grid=(grid,), in_specs=in_specs, out_specs=out_spe...]
    dot_general x8 -> x3, matrix products: 123 us -> 37.4 us  [dot(): return lax.dot_general(a, b, (dims, ((), ())), preferred_element_type=F32)]
    all_gather x3 -> x1, waiting for transfers between devices: 75.7 us -> 0.01 us  [body(): grads = lax.all_gather(gate(out_grad, None), 'dp', axis=0)]
    ppermute x0 -> x34, starting transfers between devices: none -> 60.7 us  [the longest x26 51.9 us: shift(): return lax.ppermute(x, 'dp', pairs)]
    gather x5 -> x0, local copies, waits for them, and re-layouts: 58 us -> none  [the longest x1 18.9 us: body(): back_rows[slot_index].reshape(token_count, top_count, width_local)]
  transfers between devices with their start and end apart: 9 -> 35, of which waited for: 6 -> 17; matrix products, arithmetic and copies ran while one was open for 16% -> 10% of each run, Pallas kernels for 0% -> 25%
where the time goes in v1:
time: 464 us; the launch traced here: 460 us
  waiting for transfers between devices  194 us (42%)
  Pallas kernels  129 us (28%)
  starting transfers between devices  60.7 us (13%)
  matrix products  37.4 us (8%)
  between operations  14.2 us (3%)
  other arithmetic  12.4 us (3%)
  local copies, waits for them, and re-layouts  12 us (3%)
    ppermute x26, waiting for transfers between devices, shift(): return lax.ppermute(x, 'dp', pairs)  138 us
    pallas_call x8, Pallas kernels, call(): pl.pallas_call(kernel, grid=(grid,), in_specs=in_specs, out_specs=out_spe...  97 us
    ppermute x8, waiting for transfers between devices, exchange(): parts.append(lax.ppermute(part, 'expert', pairs))  55.7 us
    ppermute x26, starting transfers between devices, shift(): return lax.ppermute(x, 'dp', pairs)  51.9 us
    dot_general x3, matrix products, dot(): return lax.dot_general(a, b, (dims, ((), ())), preferred_element_type=F32)  37.4 us
    pallas_call x4, Pallas kernels, back_call(): pl.pallas_call(kernel, grid_spec=pltpu.PrefetchScalarGridSpec(num_scalar_...  31.5 us
    unnamed x52, local copies, waits for them, and re-layouts  10.8 us
  transfers between devices with their start and end apart: 35, of which 17 were waited for; matrix products, arithmetic and copies ran while one was open for 10% of the time, Pallas kernels for 25%

profile of v1, /device:TPU:13, one launch (start us, length us, event | category | flops | bytes accessed | tf_op | source)
XLA Modules:
  0.0 459.6 jit_solution(14055511499358661892)
XLA Ops:
  9.4 1.2 fusion.5.refs_1_
  11.9 30.7 %collective-permute-done.1.refs_3_ = bf16[128,3712]{1,0:T(8,128)(2,1)S(1)} collective-permute-done((bf16[128,3712]{1,0:T(8,128)(2,1)S(1)}, bf16[128,3712]{1,0:T(8,128)(2,1)S(1)}, u32[]{:S(2)}, u32[]{:S(2)}) %collective-permute-start.1) | collective-permute-done | bytes 950304 | tf_op jit(solution)/shard_map/tok0_y/ppermute | solution.py:186
  42.6 1.4 collective-permute-start.2
  44.9 4.2 collective-permute-done.4.refs_1_
  49.1 2.4 collective-permute-start.7
  52.8 11.8 %fore0.1 = (bf16[1280,3584]{1,0:T(8,128)(2,1)}, bf16[2,320,1024]{2,1,0:T(8,128)(2,1)S(1)}, bf16[4,128,128]{2,1,0:T(8,128)(2,1)S(1)}, f32[320,128]{1,0:T(8,128)S(1)}) custom-call(s32[1]{0:T(128)} %bitcast.refs_0_, bf16[128,3712]{1,0:T(8,128)(2,1)S(1)} %fusion.5.refs_1_, bf16[128,3712]{1,0:T(8,128)(2,1)} %collective-permute-done.refs_2_, ...), custom_call_target="tpu_custom_call" | custom-call | flops 4697620 | tf_op jit(solution)/shard_map/fore0/pallas_call | solution.py:216
  66.4 11.0 %collective-permute-start.6 = (bf16[128,3712]{1,0:T(8,128)(2,1)}, bf16[128,3712]{1,0:T(8,128)(2,1)S(1)}, u32[]{:S(2)}, u32[]{:S(2)}) collective-permute-start(bf16[128,3712]{1,0:T(8,128)(2,1)} %collective-permute-done.4.refs_1_), channel_id=1, source_target_pairs={{1,0},{0,1},{3,2},{2,3},{5,4},{4,5},{7,6},{6,7},{9,8},{8,9},{11,10... | collective-permute-start | bytes 2850824 | tf_op jit(solution)/shard_map/tok1_core/ppermute | solution.py:186
  77.4 14.1 %collective-permute-done.9.refs_1_ = bf16[128,3712]{1,0:T(8,128)(2,1)S(1)} collective-permute-done((bf16[128,3712]{1,0:T(8,128)(2,1)S(1)}, bf16[128,3712]{1,0:T(8,128)(2,1)S(1)}, u32[]{:S(2)}, u32[]{:S(2)}) %collective-permute-start.9) | collective-permute-done | bytes 950304 | tf_op jit(solution)/shard_map/tok3_z/ppermute | solution.py:186
  91.4 2.6 collective-permute-start.11
  94.0 6.1 %collective-permute-start.5 = (bf16[128,3712]{1,0:T(8,128)(2,1)S(1)}, bf16[128,3712]{1,0:T(8,128)(2,1)S(1)}, u32[]{:S(2)}, u32[]{:S(2)}) collective-permute-start(bf16[128,3712]{1,0:T(8,128)(2,1)S(1)} %fusion.5.refs_1_), channel_id=1, source_target_pairs={{8,0},{9,1},{10,2},{11,3},{12,4},{13,5},{14,6},{15,7},{0,8},{1,9},... | collective-permute-start | bytes 2850824 | tf_op jit(solution)/shard_map/tok2_z/ppermute | solution.py:186
  100.1 11.8 %fore1.1 = (bf16[1280,3584]{1,0:T(8,128)(2,1)}, bf16[2,320,1024]{2,1,0:T(8,128)(2,1)S(1)}, bf16[4,128,128]{2,1,0:T(8,128)(2,1)S(1)}, f32[320,128]{1,0:T(8,128)S(1)}) custom-call(s32[1]{0:T(128)} %bitcast.refs_0_, bf16[128,3712]{1,0:T(8,128)(2,1)} %collective-permute-done.4.refs_1_, ...), custom_call_target="tpu_custom_call", output_to_operand_aliasing={{0}: (7, {})} | custom-call | flops 4697620 | tf_op jit(solution)/shard_map/fore1/pallas_call | solution.py:216
  113.5 15.9 %collective-permute-done.11.refs_3_ = bf16[128,3712]{1,0:T(8,128)(2,1)S(1)} collective-permute-done((bf16[128,3712]{1,0:T(8,128)(2,1)S(1)}, bf16[128,3712]{1,0:T(8,128)(2,1)S(1)}, u32[]{:S(2)}, u32[]{:S(2)}) %collective-permute-start.11) | collective-permute-done | bytes 950304 | tf_op jit(solution)/shard_map/tok3_y/ppermute | solution.py:186
  129.4 10.1 %collective-permute-start.10 = (bf16[128,3712]{1,0:T(8,128)(2,1)S(1)}, bf16[128,3712]{1,0:T(8,128)(2,1)S(1)}, u32[]{:S(2)}, u32[]{:S(2)}) collective-permute-start(bf16[128,3712]{1,0:T(8,128)(2,1)S(1)} %collective-permute-done.9.refs_1_), channel_id=1, source_target_pairs={{1,0},{0,1},{3,2},{2,3},{5,4},{4,5},{7,6},{6,7},{9,8},{8,9},{11,10... | collective-permute-start | bytes 2850824 | tf_op jit(solution)/shard_map/tok3_core/ppermute | solution.py:186
  139.5 42.3 %collective-permute-done.5.refs_1_ = bf16[128,3712]{1,0:T(8,128)(2,1)S(1)} collective-permute-done((bf16[128,3712]{1,0:T(8,128)(2,1)S(1)}, bf16[128,3712]{1,0:T(8,128)(2,1)S(1)}, u32[]{:S(2)}, u32[]{:S(2)}) %collective-permute-start.5) | collective-permute-done | bytes 950304 | tf_op jit(solution)/shard_map/tok2_z/ppermute | solution.py:186
  181.9 1.2 collective-permute-start.15
  183.1 11.4 %fore3.1 = (bf16[1280,3584]{1,0:T(8,128)(2,1)}, bf16[2,320,1024]{2,1,0:T(8,128)(2,1)}, bf16[4,128,128]{2,1,0:T(8,128)(2,1)S(1)}, f32[320,128]{1,0:T(8,128)S(1)}) custom-call(s32[1]{0:T(128)} %bitcast.refs_0_, bf16[128,3712]{1,0:T(8,128)(2,1)S(1)} %collective-permute-done.9.refs_1_, ...), custom_call_target="tpu_custom_call", output_to_operand_aliasing={{0}: (7, {})} | custom-call | flops 4697620 | tf_op jit(solution)/shard_map/fore3/pallas_call | solution.py:216
  194.5 6.7 %collective-permute-done.15.refs_3_ = bf16[128,3712]{1,0:T(8,128)(2,1)S(1)} collective-permute-done((bf16[128,3712]{1,0:T(8,128)(2,1)S(1)}, bf16[128,3712]{1,0:T(8,128)(2,1)S(1)}, u32[]{:S(2)}, u32[]{:S(2)}) %collective-permute-start.15) | collective-permute-done | bytes 950304 | tf_op jit(solution)/shard_map/tok2_y/ppermute | solution.py:186
  201.2 4.1 collective-permute-start.14
  207.5 1.4 collective-permute-done.16.refs_4_
  208.8 11.4 %fore2.1 = (bf16[1280,3584]{1,0:T(8,128)(2,1)}, bf16[2,320,1024]{2,1,0:T(8,128)(2,1)}, bf16[4,128,128]{2,1,0:T(8,128)(2,1)S(1)}, f32[320,128]{1,0:T(8,128)S(1)}) custom-call(s32[1]{0:T(128)} %bitcast.refs_0_, bf16[128,3712]{1,0:T(8,128)(2,1)S(1)} %collective-permute-done.5.refs_1_, ...), custom_call_target="tpu_custom_call", output_to_operand_aliasing={{0}: (7, {})} | custom-call | flops 4697620 | tf_op jit(solution)/shard_map/fore2/pallas_call | solution.py:216
  221.4 14.2 %collective-permute-done.18.refs_2_ = bf16[2,320,1024]{2,1,0:T(8,128)(2,1)} collective-permute-done((bf16[2,320,1024]{2,1,0:T(8,128)(2,1)}, bf16[2,320,1024]{2,1,0:T(8,128)(2,1)}, u32[]{:S(2)}, u32[]{:S(2)}) %collective-permute-start.18) | collective-permute-done | bytes 1310752 | tf_op jit(solution)/shard_map/fore3_x/ppermute | solution.py:200
  235.6 3.1 copy-done
  238.7 7.8 %back2.1 = (bf16[1280,3584]{1,0:T(8,128)(2,1)}, bf16[320,1024]{1,0:T(8,128)(2,1)S(1)}) custom-call(s32[4]{0:T(128)S(1)} %pad_add_fusion.3.refs_0_, bf16[16,128,3584]{2,1,0:T(8,128)(2,1)} %bitcast.51, bf16[16,128,3584]{2,1,0:T(8,128)(2,1)} %bitcast.52, bf16[16,128,3584]{2,1,0:T(8,128)(2,1)} %bitcast.53, bf16[16,128,3584]{2,1,0:T(8,128)(2,1)} %bitcast.54, ...), custom_call_target="tpu_custom_call" | custom-call | flops 2348810 | tf_op jit(solution)/shard_map/back2/pallas_call | solution.py:282
  247.9 15.8 %collective-permute-done.17.refs_2_ = bf16[2,320,1024]{2,1,0:T(8,128)(2,1)} collective-permute-done((bf16[2,320,1024]{2,1,0:T(8,128)(2,1)}, bf16[2,320,1024]{2,1,0:T(8,128)(2,1)}, u32[]{:S(2)}, u32[]{:S(2)}) %collective-permute-start.17) | collective-permute-done | bytes 1310752 | tf_op jit(solution)/shard_map/fore2_x/ppermute | solution.py:200
  263.7 3.1 copy-done.1
  266.8 8.0 %back3.1 = (bf16[1280,3584]{1,0:T(8,128)(2,1)}, bf16[320,1024]{1,0:T(8,128)(2,1)S(1)}) custom-call(s32[4]{0:T(128)S(1)} %pad_add_fusion.2.refs_0_, bf16[16,128,3584]{2,1,0:T(8,128)(2,1)} %bitcast.55, bf16[16,128,3584]{2,1,0:T(8,128)(2,1)} %bitcast.56, bf16[16,128,3584]{2,1,0:T(8,128)(2,1)} %bitcast.57, ...), custom_call_target="tpu_custom_call", output_to_operand_aliasing={{0}: (8, {})} | custom-call | flops 2348810 | tf_op jit(solution)/shard_map/back3/pallas_call | solution.py:282
  274.8 7.8 %back1.1 = (bf16[1280,3584]{1,0:T(8,128)(2,1)}, bf16[320,1024]{1,0:T(8,128)(2,1)S(1)}) custom-call(s32[4]{0:T(128)S(1)} %pad_add_fusion.1.refs_0_, bf16[16,128,3584]{2,1,0:T(8,128)(2,1)} %bitcast.59, bf16[16,128,3584]{2,1,0:T(8,128)(2,1)} %bitcast.60, bf16[16,128,3584]{2,1,0:T(8,128)(2,1)} %bitcast.61, ...), custom_call_target="tpu_custom_call", output_to_operand_aliasing={{0}: (8, {})} | custom-call | flops 2348810 | tf_op jit(solution)/shard_map/back1/pallas_call | solution.py:282
  282.7 7.8 %back0.1 = (bf16[1280,3584]{1,0:T(8,128)(2,1)}, bf16[320,1024]{1,0:T(8,128)(2,1)S(1)}) custom-call(s32[4]{0:T(128)S(1)} %pad_add_fusion.refs_0_, bf16[16,128,3584]{2,1,0:T(8,128)(2,1)} %bitcast.63, bf16[16,128,3584]{2,1,0:T(8,128)(2,1)} %bitcast.64, bf16[16,128,3584]{2,1,0:T(8,128)(2,1)} %bitcast.65, ...), custom_call_target="tpu_custom_call", output_to_operand_aliasing={{0}: (8, {})} | custom-call | flops 2348810 | tf_op jit(solution)/shard_map/back0/pallas_call | solution.py:282
  290.5 13.1 %act2.1 = (bf16[1280,1024]{1,0:T(8,128)(2,1)}, bf16[1280,1024]{1,0:T(8,128)(2,1)}, bf16[1280,1024]{1,0:T(8,128)(2,1)}, bf16[2,128,3712]{2,1,0:T(8,128)(2,1)S(1)}, bf16[2,128,3712]{2,1,0:T(8,128)(2,1)S(1)}) custom-call(s32[1]{0:T(128)} %bitcast.refs_0_, bf16[2,320,1024]{2,1,0:T(8,128)(2,1)} %get-tuple-element.92.refs_1_, ...), custom_call_target="tpu_custom_call" | custom-call | flops 4697620 | tf_op jit(solution)/shard_map/act2/pallas_call | solution.py:216
  303.6 2.2 collective-permute-start.20
  306.9 2.4 collective-permute-done.20
  309.7 12.4 %collective-permute-done.21.refs_4_ = bf16[320,1024]{1,0:T(8,128)(2,1)S(1)} collective-permute-done((bf16[320,1024]{1,0:T(8,128)(2,1)S(1)}, bf16[320,1024]{1,0:T(8,128)(2,1)S(1)}, u32[]{:S(2)}, u32[]{:S(2)}) %collective-permute-start.21) | collective-permute-done | bytes 655392 | tf_op jit(solution)/shard_map/back3_x/ppermute | solution.py:200
  323.4 13.0 %act3.1 = (bf16[1280,1024]{1,0:T(8,128)(2,1)}, bf16[1280,1024]{1,0:T(8,128)(2,1)}, bf16[1280,1024]{1,0:T(8,128)(2,1)}, bf16[2,128,3712]{2,1,0:T(8,128)(2,1)S(1)}, bf16[2,128,3712]{2,1,0:T(8,128)(2,1)S(1)}) custom-call(s32[1]{0:T(128)} %bitcast.refs_0_, ...), custom_call_target="tpu_custom_call", output_to_operand_aliasing={{0}: (9, {}), {1}: (10, {}), {2}: (11, {})} | custom-call | flops 4697620 | tf_op jit(solution)/shard_map/act3/pallas_call | solution.py:216
  338.3 5.6 %collective-permute-done.27 = bf16[128,3712]{1,0:T(8,128)(2,1)S(1)} collective-permute-done((bf16[128,3712]{1,0:T(8,128)(2,1)S(1)}, bf16[128,3712]{1,0:T(8,128)(2,1)S(1)}, u32[]{:S(2)}, u32[]{:S(2)}) %collective-permute-start.27) | collective-permute-done | bytes 950304 | tf_op jit(solution)/shard_map/sum2_y/ppermute | solution.py:186
  345.6 8.2 %collective-permute-done.23.refs_4_ = bf16[320,1024]{1,0:T(8,128)(2,1)S(1)} collective-permute-done((bf16[320,1024]{1,0:T(8,128)(2,1)S(1)}, bf16[320,1024]{1,0:T(8,128)(2,1)S(1)}, u32[]{:S(2)}, u32[]{:S(2)}) %collective-permute-start.23) | collective-permute-done | bytes 655392 | tf_op jit(solution)/shard_map/back1_x/ppermute | solution.py:200
  354.0 12.1 %act1.1 = (bf16[1280,1024]{1,0:T(8,128)(2,1)}, bf16[1280,1024]{1,0:T(8,128)(2,1)}, bf16[1280,1024]{1,0:T(8,128)(2,1)}, bf16[2,128,3712]{2,1,0:T(8,128)(2,1)S(1)}, bf16[2,128,3712]{2,1,0:T(8,128)(2,1)S(1)}) custom-call(s32[1]{0:T(128)} %bitcast.refs_0_, ...), custom_call_target="tpu_custom_call", output_to_operand_aliasing={{0}: (9, {}), {1}: (10, {}), {2}: (11, {})} | custom-call | flops 4697620 | tf_op jit(solution)/shard_map/act1/pallas_call | solution.py:216
  368.4 3.2 collective-permute-start.33
  371.6 4.0 collective-permute-done.28
  376.8 1.8 fusion.11
  378.6 5.1 %collective-permute-done.25.refs_4_ = bf16[320,1024]{1,0:T(8,128)(2,1)S(1)} collective-permute-done((bf16[320,1024]{1,0:T(8,128)(2,1)S(1)}, bf16[320,1024]{1,0:T(8,128)(2,1)S(1)}, u32[]{:S(2)}, u32[]{:S(2)}) %collective-permute-start.25) | collective-permute-done | bytes 655392 | tf_op jit(solution)/shard_map/back0_x/ppermute | solution.py:200
  383.7 1.2 collective-permute-start.29
  384.9 12.5 %act0.1 = (bf16[1280,1024]{1,0:T(8,128)(2,1)}, bf16[1280,1024]{1,0:T(8,128)(2,1)}, bf16[1280,1024]{1,0:T(8,128)(2,1)}, bf16[2,128,3712]{2,1,0:T(8,128)(2,1)S(1)}, bf16[2,128,3712]{2,1,0:T(8,128)(2,1)S(1)}) custom-call(s32[1]{0:T(128)} %bitcast.refs_0_, ...), custom_call_target="tpu_custom_call", output_to_operand_aliasing={{0}: (9, {}), {1}: (10, {}), {2}: (11, {})} | custom-call | flops 4697620 | tf_op jit(solution)/shard_map/act0/pallas_call | solution.py:216
  398.5 13.7 %fusion.1 = bf16[1,3584,1024]{2,1,0:T(8,128)(2,1)} fusion(bf16[1280,3584]{1,0:T(8,128)(2,1)S(1)} %bitcast.68, bf16[1280,1024]{1,0:T(8,128)(2,1)} %get-tuple-element.141), kind=kOutput, calls=%fused_computation.4 | convolution fusion | flops 9398910976 | bytes 19136512 | tf_op jit(solution)/shard_map/dot_general | solution.py:34
  412.1 11.8 %fusion.2 = bf16[1,3584,1024]{2,1,0:T(8,128)(2,1)} fusion(bf16[1280,3584]{1,0:T(8,128)(2,1)S(1)} %bitcast.68, bf16[1280,1024]{1,0:T(8,128)(2,1)S(1)} %copy-done.17), kind=kOutput, calls=%fused_computation.5 | convolution fusion | flops 9398910976 | bytes 19136512 | tf_op jit(solution)/shard_map/dot_general | solution.py:34
  424.0 1.5 add_convert_fusion
  427.2 11.9 %fusion = bf16[1,1024,3584]{2,1,0:T(8,128)(2,1)} fusion(bf16[1280,1024]{1,0:T(8,128)(2,1)S(1)} %copy-done.16, bf16[1280,3584]{1,0:T(8,128)(2,1)S(1)} %bitcast.70), kind=kOutput, calls=%fused_computation.3 | convolution fusion | flops 9398910976 | bytes 19136512 | tf_op jit(solution)/shard_map/dot_general | solution.py:34
  439.2 9.7 %collective-permute-done.31 = bf16[128,3712]{1,0:T(8,128)(2,1)S(1)} collective-permute-done((bf16[128,3712]{1,0:T(8,128)(2,1)S(1)}, bf16[128,3712]{1,0:T(8,128)(2,1)S(1)}, u32[]{:S(2)}, u32[]{:S(2)}) %collective-permute-start.31) | collective-permute-done | bytes 950304 | tf_op jit(solution)/shard_map/sum1_z/ppermute | solution.py:186
  448.9 2.2 convert_add_fusion.1
  (112 shorter events, 28.5 us)
Async XLA Ops:
  7.2 228.5 %all-gather.3.cloned.1.call-start = ((), (), s32[]{:S(2)}) async-start(), calls=%async_computation | async-start | bytes 15597568 | tf_op jit(solution)/shard_map/all_gather | solution.py:389
  10.7 31.9 %collective-permute-start.1 = (bf16[128,3712]{1,0:T(8,128)(2,1)S(1)}, bf16[128,3712]{1,0:T(8,128)(2,1)S(1)}, u32[]{:S(2)}, u32[]{:S(2)}) collective-permute-start(bf16[128,3712]{1,0:T(8,128)(2,1)S(1)} %fusion.5.refs_1_), channel_id=1, source_target_pairs={{2,0},{3,1},{0,2},{1,3},{6,4},{7,5},{4,6},{5,7},{10,8},{11,9},{8,1... | collective-permute-start | bytes 2850824 | tf_op jit(solution)/shard_map/tok0_y/ppermute | solution.py:186
  10.9 38.2 %collective-permute-start.4 = (bf16[128,3712]{1,0:T(8,128)(2,1)S(1)}, bf16[128,3712]{1,0:T(8,128)(2,1)}, u32[]{:S(2)}, u32[]{:S(2)}) collective-permute-start(bf16[128,3712]{1,0:T(8,128)(2,1)S(1)} %fusion.5.refs_1_), channel_id=1, source_target_pairs={{4,0},{5,1},{6,2},{7,3},{8,4},{9,5},{10,6},{11,7},{12,8},{13,9},{1... | collective-permute-start | bytes 2850824 | tf_op jit(solution)/shard_map/tok1_z/ppermute | solution.py:186
  11.0 40.6 %collective-permute-start = (bf16[128,3712]{1,0:T(8,128)(2,1)S(1)}, bf16[128,3712]{1,0:T(8,128)(2,1)}, u32[]{:S(2)}, u32[]{:S(2)}) collective-permute-start(bf16[128,3712]{1,0:T(8,128)(2,1)S(1)} %fusion.5.refs_1_), channel_id=1, source_target_pairs={{1,0},{0,1},{3,2},{2,3},{5,4},{4,5},{7,6},{6,7},{9,8},{8,9},{11,10... | collective-permute-start | bytes 2850824 | tf_op jit(solution)/shard_map/tok0_core/ppermute | solution.py:186
  42.6 9.0 %collective-permute-start.2 = (bf16[128,3712]{1,0:T(8,128)(2,1)S(1)}, bf16[128,3712]{1,0:T(8,128)(2,1)}, u32[]{:S(2)}, u32[]{:S(2)}) collective-permute-start(bf16[128,3712]{1,0:T(8,128)(2,1)S(1)} %collective-permute-done.1.refs_3_), channel_id=1, source_target_pairs={{1,0},{0,1},{3,2},{2,3},{5,4},{4,5},{7,6},{6,7},{9,8},{8,9},{11,10... | collective-permute-start | bytes 2850824 | tf_op jit(solution)/shard_map/tok0_core/ppermute | solution.py:186
  49.1 17.3 %collective-permute-start.7 = (bf16[128,3712]{1,0:T(8,128)(2,1)}, bf16[128,3712]{1,0:T(8,128)(2,1)}, u32[]{:S(2)}, u32[]{:S(2)}) collective-permute-start(bf16[128,3712]{1,0:T(8,128)(2,1)} %collective-permute-done.4.refs_1_), channel_id=1, source_target_pairs={{2,0},{3,1},{0,2},{1,3},{6,4},{7,5},{4,6},{5,7},{10,8},{11,9},{8,1... | collective-permute-start | bytes 2850824 | tf_op jit(solution)/shard_map/tok1_y/ppermute | solution.py:186
  51.5 39.9 %collective-permute-start.9 = (bf16[128,3712]{1,0:T(8,128)(2,1)S(1)}, bf16[128,3712]{1,0:T(8,128)(2,1)S(1)}, u32[]{:S(2)}, u32[]{:S(2)}) collective-permute-start(bf16[128,3712]{1,0:T(8,128)(2,1)S(1)} %fusion.5.refs_1_), channel_id=1, source_target_pairs={{12,0},{13,1},{14,2},{15,3},{0,4},{1,5},{2,6},{3,7},{4,8},{5,9},{6... | collective-permute-start | bytes 2850824 | tf_op jit(solution)/shard_map/tok3_z/ppermute | solution.py:186
  65.2 64.2 %collective-permute-start.3 = (bf16[2,320,1024]{2,1,0:T(8,128)(2,1)S(1)}, bf16[2,320,1024]{2,1,0:T(8,128)(2,1)S(1)}, u32[]{:S(2)}, u32[]{:S(2)}) collective-permute-start(bf16[2,320,1024]{2,1,0:T(8,128)(2,1)S(1)} %get-tuple-element.74.refs_1_), channel_id=1, source_target_pairs={{16,0},{0,16},{17,1},{1,17},{18,2},{2,18},{19,3},{3,19},{20,4},{4,... | collective-permute-start | bytes 3932168 | tf_op jit(solution)/shard_map/fore0_x/ppermute | solution.py:200
  66.4 33.7 %collective-permute-start.6 = (bf16[128,3712]{1,0:T(8,128)(2,1)}, bf16[128,3712]{1,0:T(8,128)(2,1)S(1)}, u32[]{:S(2)}, u32[]{:S(2)}) collective-permute-start(bf16[128,3712]{1,0:T(8,128)(2,1)} %collective-permute-done.4.refs_1_), channel_id=1, source_target_pairs={{1,0},{0,1},{3,2},{2,3},{5,4},{4,5},{7,6},{6,7},{9,8},{8,9},{11,10... | collective-permute-start | bytes 2850824 | tf_op jit(solution)/shard_map/tok1_core/ppermute | solution.py:186
  77.4 22.7 %collective-permute-start.8 = (bf16[128,3712]{1,0:T(8,128)(2,1)}, bf16[128,3712]{1,0:T(8,128)(2,1)S(1)}, u32[]{:S(2)}, u32[]{:S(2)}) collective-permute-start(bf16[128,3712]{1,0:T(8,128)(2,1)} %collective-permute-done.7.refs_3_), channel_id=1, source_target_pairs={{1,0},{0,1},{3,2},{2,3},{5,4},{4,5},{7,6},{6,7},{9,8},{8,9},{11,10... | collective-permute-start | bytes 2850824 | tf_op jit(solution)/shard_map/tok1_core/ppermute | solution.py:186
  91.4 37.9 %collective-permute-start.11 = (bf16[128,3712]{1,0:T(8,128)(2,1)S(1)}, bf16[128,3712]{1,0:T(8,128)(2,1)S(1)}, u32[]{:S(2)}, u32[]{:S(2)}) collective-permute-start(bf16[128,3712]{1,0:T(8,128)(2,1)S(1)} %collective-permute-done.9.refs_1_), channel_id=1, source_target_pairs={{2,0},{3,1},{0,2},{1,3},{6,4},{7,5},{4,6},{5,7},{10,8},{11,9},{8,1... | collective-permute-start | bytes 2850824 | tf_op jit(solution)/shard_map/tok3_y/ppermute | solution.py:186
  94.0 87.9 %collective-permute-start.5 = (bf16[128,3712]{1,0:T(8,128)(2,1)S(1)}, bf16[128,3712]{1,0:T(8,128)(2,1)S(1)}, u32[]{:S(2)}, u32[]{:S(2)}) collective-permute-start(bf16[128,3712]{1,0:T(8,128)(2,1)S(1)} %fusion.5.refs_1_), channel_id=1, source_target_pairs={{8,0},{9,1},{10,2},{11,3},{12,4},{13,5},{14,6},{15,7},{0,8},{1,9},... | collective-permute-start | bytes 2850824 | tf_op jit(solution)/shard_map/tok2_z/ppermute | solution.py:186
  112.6 81.9 %copy-start.4 = (bf16[2,320,1024]{2,1,0:T(8,128)(2,1)}, bf16[2,320,1024]{2,1,0:T(8,128)(2,1)S(1)}, u32[]{:S(2)}) copy-start(bf16[2,320,1024]{2,1,0:T(8,128)(2,1)S(1)} %get-tuple-element.87.refs_1_) | copy-start | bytes 3932164
  112.6 88.7 %collective-permute-start.13 = (bf16[2,320,1024]{2,1,0:T(8,128)(2,1)S(1)}, bf16[2,320,1024]{2,1,0:T(8,128)(2,1)S(1)}, u32[]{:S(2)}, u32[]{:S(2)}) collective-permute-start(bf16[2,320,1024]{2,1,0:T(8,128)(2,1)S(1)} %get-tuple-element.87.refs_1_), channel_id=1, source_target_pairs={{16,0},{0,16},{17,1},{1,17},{18,2},{2,18},{19,3},{3,19},{20,4},{4,... | collective-permute-start | bytes 3932168 | tf_op jit(solution)/shard_map/fore1_x/ppermute | solution.py:200
  129.4 65.1 %copy-start.2 = (bf16[2,320,1024]{2,1,0:T(8,128)(2,1)}, bf16[2,320,1024]{2,1,0:T(8,128)(2,1)S(1)}, u32[]{:S(2)}) copy-start(bf16[2,320,1024]{2,1,0:T(8,128)(2,1)S(1)} %collective-permute-done.3.refs_2_) | copy-start | bytes 3932164
  129.4 53.7 %collective-permute-start.10 = (bf16[128,3712]{1,0:T(8,128)(2,1)S(1)}, bf16[128,3712]{1,0:T(8,128)(2,1)S(1)}, u32[]{:S(2)}, u32[]{:S(2)}) collective-permute-start(bf16[128,3712]{1,0:T(8,128)(2,1)S(1)} %collective-permute-done.9.refs_1_), channel_id=1, source_target_pairs={{1,0},{0,1},{3,2},{2,3},{5,4},{4,5},{7,6},{6,7},{9,8},{8,9},{11,10... | collective-permute-start | bytes 2850824 | tf_op jit(solution)/shard_map/tok3_core/ppermute | solution.py:186
  139.4 43.7 %collective-permute-start.12 = (bf16[128,3712]{1,0:T(8,128)(2,1)S(1)}, bf16[128,3712]{1,0:T(8,128)(2,1)S(1)}, u32[]{:S(2)}, u32[]{:S(2)}) collective-permute-start(bf16[128,3712]{1,0:T(8,128)(2,1)S(1)} %collective-permute-done.11.refs_3_), channel_id=1, source_target_pairs={{1,0},{0,1},{3,2},{2,3},{5,4},{4,5},{7,6},{6,7},{9,8},{8,9},{11,10... | collective-permute-start | bytes 2850824 | tf_op jit(solution)/shard_map/tok3_core/ppermute | solution.py:186
  181.9 19.4 %collective-permute-start.15 = (bf16[128,3712]{1,0:T(8,128)(2,1)S(1)}, bf16[128,3712]{1,0:T(8,128)(2,1)S(1)}, u32[]{:S(2)}, u32[]{:S(2)}) collective-permute-start(bf16[128,3712]{1,0:T(8,128)(2,1)S(1)} %collective-permute-done.5.refs_1_), channel_id=1, source_target_pairs={{2,0},{3,1},{0,2},{1,3},{6,4},{7,5},{4,6},{5,7},{10,8},{11,9},{8,1... | collective-permute-start | bytes 2850824 | tf_op jit(solution)/shard_map/tok2_y/ppermute | solution.py:186
  194.5 69.2 %copy-start.14 = (bf16[4,128,128]{2,1,0:T(8,128)(2,1)}, bf16[4,128,128]{2,1,0:T(8,128)(2,1)S(1)}, u32[]{:S(2)}) copy-start(bf16[4,128,128]{2,1,0:T(8,128)(2,1)S(1)} %get-tuple-element.98.refs_5_) | copy-start | bytes 393220
  201.2 19.0 %copy-start.6 = (bf16[2,320,1024]{2,1,0:T(8,128)(2,1)}, bf16[2,320,1024]{2,1,0:T(8,128)(2,1)S(1)}, u32[]{:S(2)}) copy-start(bf16[2,320,1024]{2,1,0:T(8,128)(2,1)S(1)} %collective-permute-done.13.refs_2_) | copy-start | bytes 3932164
  201.2 6.2 %collective-permute-start.14 = (bf16[128,3712]{1,0:T(8,128)(2,1)S(1)}, bf16[128,3712]{1,0:T(8,128)(2,1)S(1)}, u32[]{:S(2)}, u32[]{:S(2)}) collective-permute-start(bf16[128,3712]{1,0:T(8,128)(2,1)S(1)} %collective-permute-done.5.refs_1_), channel_id=1, source_target_pairs={{1,0},{0,1},{3,2},{2,3},{5,4},{4,5},{7,6},{6,7},{9,8},{8,9},{11,10... | collective-permute-start | bytes 2850824 | tf_op jit(solution)/shard_map/tok2_core/ppermute | solution.py:186
  205.3 3.5 collective-permute-start.16
  205.4 30.2 %collective-permute-start.18 = (bf16[2,320,1024]{2,1,0:T(8,128)(2,1)}, bf16[2,320,1024]{2,1,0:T(8,128)(2,1)}, u32[]{:S(2)}, u32[]{:S(2)}) collective-permute-start(bf16[2,320,1024]{2,1,0:T(8,128)(2,1)} %get-tuple-element.100.refs_1_), channel_id=1, source_target_pairs={{16,0},{0,16},{17,1},{1,17},{18,2},{2,18},{19,3},{3,19},{20,4},{4,... | collective-permute-start | bytes 3932168 | tf_op jit(solution)/shard_map/fore3_x/ppermute | solution.py:200
  220.2 43.5 %collective-permute-start.17 = (bf16[2,320,1024]{2,1,0:T(8,128)(2,1)}, bf16[2,320,1024]{2,1,0:T(8,128)(2,1)}, u32[]{:S(2)}, u32[]{:S(2)}) collective-permute-start(bf16[2,320,1024]{2,1,0:T(8,128)(2,1)} %get-tuple-element.92.refs_1_), channel_id=1, source_target_pairs={{16,0},{0,16},{17,1},{1,17},{18,2},{2,18},{19,3},{3,19},{20,4},{4,... | collective-permute-start | bytes 3932168 | tf_op jit(solution)/shard_map/fore2_x/ppermute | solution.py:200
  246.6 43.9 %collective-permute-start.19 = (bf16[320,1024]{1,0:T(8,128)(2,1)S(1)}, bf16[320,1024]{1,0:T(8,128)(2,1)}, u32[]{:S(2)}, u32[]{:S(2)}) collective-permute-start(bf16[320,1024]{1,0:T(8,128)(2,1)S(1)} %get-tuple-element.112.refs_3_), channel_id=1, source_target_pairs={{16,0},{0,16},{17,1},{1,17},{18,2},{2,18},{19,3},{3,19},{20,4},{4,... | collective-permute-start | bytes 1966088 | tf_op jit(solution)/shard_map/back2_x/ppermute | solution.py:200
  303.6 5.7 %collective-permute-start.20 = (bf16[2,128,3712]{2,1,0:T(8,128)(2,1)S(1)}, bf16[2,128,3712]{2,1,0:T(8,128)(2,1)S(1)}, u32[]{:S(2)}, u32[]{:S(2)}) collective-permute-start(bf16[2,128,3712]{2,1,0:T(8,128)(2,1)S(1)} %get-tuple-element.114), channel_id=1, source_target_pairs={{1,0},{0,1},{3,2},{2,3},{5,4},{4,5},{7,6},{6,7},{9,8},{8,9},{11,10... | collective-permute-start | bytes 5701640 | tf_op jit(solution)/shard_map/sum2_core/ppermute | solution.py:186
  305.8 16.4 %collective-permute-start.21 = (bf16[320,1024]{1,0:T(8,128)(2,1)S(1)}, bf16[320,1024]{1,0:T(8,128)(2,1)S(1)}, u32[]{:S(2)}, u32[]{:S(2)}) collective-permute-start(bf16[320,1024]{1,0:T(8,128)(2,1)S(1)} %get-tuple-element.115.refs_3_), channel_id=1, source_target_pairs={{16,0},{0,16},{17,1},{1,17},{18,2},{2,18},{19,3},{3,19},{20,4},{4,... | collective-permute-start | bytes 1966088 | tf_op jit(solution)/shard_map/back3_x/ppermute | solution.py:200
  309.3 14.1 %copy-start.15 = (bf16[4,128,128]{2,1,0:T(8,128)(2,1)S(1)}, bf16[4,128,128]{2,1,0:T(8,128)(2,1)}, u32[]{:S(2)}) copy-start(bf16[4,128,128]{2,1,0:T(8,128)(2,1)} %copy-done.14) | copy-start | bytes 393220
  322.1 21.8 %collective-permute-start.27 = (bf16[128,3712]{1,0:T(8,128)(2,1)S(1)}, bf16[128,3712]{1,0:T(8,128)(2,1)S(1)}, u32[]{:S(2)}, u32[]{:S(2)}) collective-permute-start(bf16[128,3712]{1,0:T(8,128)(2,1)S(1)} %get-tuple-element.137), channel_id=1, source_target_pairs={{2,0},{3,1},{0,2},{1,3},{6,4},{7,5},{4,6},{5,7},{10,8},{11,9},{8,1... | collective-permute-start | bytes 2850824 | tf_op jit(solution)/shard_map/sum2_y/ppermute | solution.py:186
  336.3 8.8 %collective-permute-start.22 = (bf16[2,128,3712]{2,1,0:T(8,128)(2,1)S(1)}, bf16[2,128,3712]{2,1,0:T(8,128)(2,1)S(1)}, u32[]{:S(2)}, u32[]{:S(2)}) collective-permute-start(bf16[2,128,3712]{2,1,0:T(8,128)(2,1)S(1)} %get-tuple-element.120), channel_id=1, source_target_pairs={{1,0},{0,1},{3,2},{2,3},{5,4},{4,5},{7,6},{6,7},{9,8},{8,9},{11,10... | collective-permute-start | bytes 5701640 | tf_op jit(solution)/shard_map/sum3_core/ppermute | solution.py:186
  337.4 16.4 %collective-permute-start.23 = (bf16[320,1024]{1,0:T(8,128)(2,1)S(1)}, bf16[320,1024]{1,0:T(8,128)(2,1)S(1)}, u32[]{:S(2)}, u32[]{:S(2)}) collective-permute-start(bf16[320,1024]{1,0:T(8,128)(2,1)S(1)} %get-tuple-element.121.refs_3_), channel_id=1, source_target_pairs={{16,0},{0,16},{17,1},{1,17},{18,2},{2,18},{19,3},{3,19},{20,4},{4,... | collective-permute-start | bytes 1966088 | tf_op jit(solution)/shard_map/back1_x/ppermute | solution.py:200
  353.8 21.9 %collective-permute-start.28 = (bf16[128,3712]{1,0:T(8,128)(2,1)S(1)}, bf16[128,3712]{1,0:T(8,128)(2,1)S(1)}, u32[]{:S(2)}, u32[]{:S(2)}) collective-permute-start(bf16[128,3712]{1,0:T(8,128)(2,1)S(1)} %get-tuple-element.138), channel_id=1, source_target_pairs={{2,0},{3,1},{0,2},{1,3},{6,4},{7,5},{4,6},{5,7},{10,8},{11,9},{8,1... | collective-permute-start | bytes 2850824 | tf_op jit(solution)/shard_map/sum3_y/ppermute | solution.py:186
  366.2 10.7 %collective-permute-start.24 = (bf16[2,128,3712]{2,1,0:T(8,128)(2,1)S(1)}, bf16[2,128,3712]{2,1,0:T(8,128)(2,1)S(1)}, u32[]{:S(2)}, u32[]{:S(2)}) collective-permute-start(bf16[2,128,3712]{2,1,0:T(8,128)(2,1)S(1)} %get-tuple-element.126), channel_id=1, source_target_pairs={{1,0},{0,1},{3,2},{2,3},{5,4},{4,5},{7,6},{6,7},{9,8},{8,9},{11,10... | collective-permute-start | bytes 5701640 | tf_op jit(solution)/shard_map/sum1_core/ppermute | solution.py:186
  367.3 16.4 %collective-permute-start.25 = (bf16[320,1024]{1,0:T(8,128)(2,1)S(1)}, bf16[320,1024]{1,0:T(8,128)(2,1)S(1)}, u32[]{:S(2)}, u32[]{:S(2)}) collective-permute-start(bf16[320,1024]{1,0:T(8,128)(2,1)S(1)} %get-tuple-element.127.refs_3_), channel_id=1, source_target_pairs={{16,0},{0,16},{17,1},{1,17},{18,2},{2,18},{19,3},{3,19},{20,4},{4,... | collective-permute-start | bytes 1966088 | tf_op jit(solution)/shard_map/back0_x/ppermute | solution.py:200
  368.4 70.7 %collective-permute-start.33 = (bf16[128,3712]{1,0:T(8,128)(2,1)}, bf16[128,3712]{1,0:T(8,128)(2,1)}, u32[]{:S(2)}, u32[]{:S(2)}) collective-permute-start(bf16[128,3712]{1,0:T(8,128)(2,1)} %add_convert_fusion.2), channel_id=1, source_target_pairs={{8,0},{9,1},{10,2},{11,3},{12,4},{13,5},{14,6},{15,7},{0,8},{1,9},... | collective-permute-start | bytes 2850824 | tf_op jit(solution)/shard_map/sum2_z/ppermute | solution.py:186
  376.8 62.4 %collective-permute-start.32 = (bf16[128,3712]{1,0:T(8,128)(2,1)}, bf16[128,3712]{1,0:T(8,128)(2,1)}, u32[]{:S(2)}, u32[]{:S(2)}) collective-permute-start(bf16[128,3712]{1,0:T(8,128)(2,1)} %add_convert_fusion.1), channel_id=1, source_target_pairs={{4,0},{5,1},{6,2},{7,3},{8,4},{9,5},{10,6},{11,7},{12,8},{13,9},{1... | collective-permute-start | bytes 2850824 | tf_op jit(solution)/shard_map/sum3_z/ppermute | solution.py:186
  376.8 21.6 %slice-start = ((s8[9175040]{0:T(1024)(128)(4,1)}), s8[4194304]{0:T(1024)(128)(4,1)S(1)}, s32[]{:S(2)}) async-start(s8[9175040]{0:T(1024)(128)(4,1)} %bitcast.67), calls=%async_computation.1 | async-start | bytes 8388608
  383.7 40.3 %collective-permute-start.29 = (bf16[128,3712]{1,0:T(8,128)(2,1)}, bf16[128,3712]{1,0:T(8,128)(2,1)}, u32[]{:S(2)}, u32[]{:S(2)}) collective-permute-start(bf16[128,3712]{1,0:T(8,128)(2,1)} %get-tuple-element.139), channel_id=1, source_target_pairs={{2,0},{3,1},{0,2},{1,3},{6,4},{7,5},{4,6},{5,7},{10,8},{11,9},{8,1... | collective-permute-start | bytes 2850824 | tf_op jit(solution)/shard_map/sum1_y/ppermute | solution.py:186
  384.9 13.5 %slice-start.1 = ((s8[9175040]{0:T(1024)(128)(4,1)}), s8[4194304]{0:T(1024)(128)(4,1)S(1)}, s32[]{:S(2)}) async-start(s8[9175040]{0:T(1024)(128)(4,1)} %bitcast.67), calls=%async_computation.2 | async-start | bytes 8388608
  384.9 13.5 %slice-start.2 = ((s8[9175040]{0:T(1024)(128)(4,1)}), s8[786432]{0:T(1024)(128)(4,1)S(1)}, s32[]{:S(2)}) async-start(s8[9175040]{0:T(1024)(128)(4,1)} %bitcast.67), calls=%async_computation.3 | async-start | bytes 1572864
  397.4 28.1 %collective-permute-start.26 = (bf16[2,128,3712]{2,1,0:T(8,128)(2,1)S(1)}, bf16[2,128,3712]{2,1,0:T(8,128)(2,1)S(1)}, u32[]{:S(2)}, u32[]{:S(2)}) collective-permute-start(bf16[2,128,3712]{2,1,0:T(8,128)(2,1)S(1)} %get-tuple-element.132), channel_id=1, source_target_pairs={{1,0},{0,1},{3,2},{2,3},{5,4},{4,5},{7,6},{6,7},{9,8},{8,9},{11,10... | collective-permute-start | bytes 5701640 | tf_op jit(solution)/shard_map/sum0_core/ppermute | solution.py:186
  398.4 13.7 %copy-start.17 = (bf16[1280,1024]{1,0:T(8,128)(2,1)S(1)}, bf16[1280,1024]{1,0:T(8,128)(2,1)}, u32[]{:S(2)}) copy-start(bf16[1280,1024]{1,0:T(8,128)(2,1)} %get-tuple-element.142) | copy-start | bytes 7864324
  398.5 27.6 %slice-start.3 = ((s8[9175040]{0:T(1024)(128)(4,1)}), s8[4194304]{0:T(1024)(128)(4,1)S(1)}, s32[]{:S(2)}) async-start(s8[9175040]{0:T(1024)(128)(4,1)} %bitcast.69), calls=%async_computation.4 | async-start | bytes 8388608
  398.5 27.6 %slice-start.4 = ((s8[9175040]{0:T(1024)(128)(4,1)}), s8[4194304]{0:T(1024)(128)(4,1)S(1)}, s32[]{:S(2)}) async-start(s8[9175040]{0:T(1024)(128)(4,1)} %bitcast.69), calls=%async_computation.5 | async-start | bytes 8388608
  412.1 11.8 %copy-start.18 = (bf16[128,3712]{1,0:T(8,128)(2,1)S(1)}, bf16[128,3712]{1,0:T(8,128)(2,1)}, u32[]{:S(2)}) copy-start(bf16[128,3712]{1,0:T(8,128)(2,1)} %get-tuple-element.134) | copy-start | bytes 2850820
  412.1 14.0 %slice-start.5 = ((s8[9175040]{0:T(1024)(128)(4,1)}), s8[786432]{0:T(1024)(128)(4,1)S(1)}, s32[]{:S(2)}) async-start(s8[9175040]{0:T(1024)(128)(4,1)} %bitcast.69), calls=%async_computation.6 | async-start | bytes 1572864
  425.5 23.4 %collective-permute-start.31 = (bf16[128,3712]{1,0:T(8,128)(2,1)S(1)}, bf16[128,3712]{1,0:T(8,128)(2,1)S(1)}, u32[]{:S(2)}, u32[]{:S(2)}) collective-permute-start(bf16[128,3712]{1,0:T(8,128)(2,1)S(1)} %add_convert_fusion), channel_id=1, source_target_pairs={{12,0},{13,1},{14,2},{15,3},{0,4},{1,5},{2,6},{3,7},{4,8},{5,9},{6... | collective-permute-start | bytes 2850824 | tf_op jit(solution)/shard_map/sum1_z/ppermute | solution.py:186
  425.8 23.1 %collective-permute-start.30 = (bf16[128,3712]{1,0:T(8,128)(2,1)S(1)}, bf16[128,3712]{1,0:T(8,128)(2,1)S(1)}, u32[]{:S(2)}, u32[]{:S(2)}) collective-permute-start(bf16[128,3712]{1,0:T(8,128)(2,1)S(1)} %fusion.10), channel_id=1, source_target_pairs={{2,0},{3,1},{0,2},{1,3},{6,4},{7,5},{4,6},{5,7},{10,8},{11,9},{8,1... | collective-permute-start | bytes 2850824 | tf_op jit(solution)/shard_map/sum0_y/ppermute | solution.py:186
  (13 other events, 54.2 us)
Sparse Core Ops, SparseCore 0:
  10.3 173.5 all-gather.2

commit v2 on v1

--- a/solution.py
+++ b/solution.py
@@ -53,21 +53,21 @@
 
 
 def fore_kernel(n, slots, top, width, step_cols, *refs):
-    me_ref, block_refs = refs[0], refs[1 : 1 + n]
-    gate_ref, up_ref = refs[1 + n : 3 + n]
+    me_ref, block_refs = refs[1], refs[2 : 2 + n]
+    gate_ref, up_ref = refs[2 + n : 4 + n]
     rows_ref, part_ref, pick_ref, scale_ref = refs[-4:]
 
     @pl.when(pl.program_id(0) == 0)
     def _():
         me = me_ref[0].astype(F32)
-        count = block_refs[0].shape[0]
+        count = block_refs[0].shape[1]
         lower = (
             lax.broadcasted_iota(jnp.int32, (count, count), 1)
             < lax.broadcasted_iota(jnp.int32, (count, count), 0)
         ).astype(BF16)
         lane = lax.broadcasted_iota(jnp.int32, (count, LANES), 1).astype(F32)
         for b in range(n):
-            meta = block_refs[b][:, width : width + LANES].astype(F32)
+            meta = block_refs[b][0, :, width : width + LANES].astype(F32)
             hit = (meta[:, :top] == me).astype(F32)
             chosen = jnp.max(hit, axis=1, keepdims=True)
             weight = jnp.sum(hit * meta[:, top : 2 * top], axis=1, keepdims=True)
@@ -80,7 +80,7 @@
             scale_ref[at, :] = dot(pick, jnp.broadcast_to(weight, (count, LANES)).astype(BF16))
             for left in range(0, width, step_cols):
                 cols = slice(left, left + step_cols)
-                rows_ref[at, cols] = dot(pick, block_refs[b][:, cols]).astype(BF16)
+                rows_ref[at, cols] = dot(pick, block_refs[b][0, :, cols]).astype(BF16)
 
     rows = rows_ref[...]
     part_ref[0] = dot(rows, gate_ref[0]).astype(BF16)
@@ -166,6 +166,7 @@
     n_out, n_in, n_core = split_dp(groups)
     me = lax.axis_index("dp")
     me_arr = me.astype(jnp.int32).reshape(1)
+    place = (me // (n_in * n_core), (me // n_core) % n_in, me % n_core)
     sizes = (n_out, n_in, n_core)
     members = n_in * n_core
     rows = members * slots
@@ -189,7 +190,7 @@
         at = (me // (n_in * n_core) + r) % n_out, (me // n_core + i) % n_in, (me + c) % n_core
         return ((at[0] * n_in + at[1]) * n_core + at[2]).astype(jnp.int32)
 
-    near = sorted(range(n_out), key=lambda r: (min(r, n_out - r), r))
+    near = [0] + sorted(range(1, n_out), key=lambda r: (-min(r, n_out - r), r))
     far = near[::-1]
 
     def exchange(part, name):
@@ -232,32 +233,46 @@
     unit_tile = tile_of(units, 256)
     all_rows = n_out * rows
 
-    def fore_call(r, blocks, before):
+    def fore_call(r, blocks, places, before):
         def kernel(*refs):
-            fore_kernel(members, slots, top_count, width, step_cols, *refs[: 3 + members], *refs[-4:])
-
-        weight = pl.BlockSpec((1, width, unit_tile), lambda j: (0, 0, j))
-        return call(
+            fore_kernel(members, slots, top_count, width, step_cols, *refs[: 4 + members], *refs[-4:])
+
+        ins = [jnp.stack(places), me_arr, *blocks, gate_weight, up_weight]
+        in_specs = [smem]
+        in_specs += [
+            pl.BlockSpec((1, *blocks[b].shape[1:]), lambda j, at, b=b: (at[b], 0, 0))
+            for b in range(members)
+        ]
+        in_specs += [pl.BlockSpec((1, width, unit_tile), lambda j, at: (0, 0, j))] * 2
+        aliases = {}
+        if before is not None:
+            aliases[len(ins)] = 0
+            ins.append(before[0])
+            in_specs.append(anywhere)
+        return pl.pallas_call(
             kernel,
-            f"fore{r}",
-            units // unit_tile,
-            [me_arr, *blocks, gate_weight, up_weight],
-            [smem, *[whole(b.shape) for b in blocks], weight, weight],
-            [
+            grid_spec=pltpu.PrefetchScalarGridSpec(
+                num_scalar_prefetch=1,
+                grid=(units // unit_tile,),
+                in_specs=in_specs,
+                out_specs=[
+                    pl.BlockSpec((rows, width), lambda j, at: (r, 0)),
+                    pl.BlockSpec((2, rows, unit_tile), lambda j, at: (0, 0, j)),
+                    whole((members, token_count, LANES)),
+                    whole((rows, LANES)),
+                ],
+            ),
+            out_shape=[
                 sds((all_rows, width)),
                 sds((2, rows, units)),
                 sds((members, token_count, LANES)),
                 sds((rows, LANES), F32),
             ],
-            [
-                at_rows(r, width),
-                pl.BlockSpec((2, rows, unit_tile), lambda j: (0, 0, j)),
-                whole((members, token_count, LANES)),
-                whole((rows, LANES)),
-            ],
-            before,
-            2 * rows * width * 2 * units,
-        )
+            input_output_aliases=aliases,
+            compiler_params=pltpu.CompilerParams(vmem_limit_bytes=VMEM_LIMIT),
+            cost_estimate=cost(4 * rows * width * units // 1000, 0),
+            name=f"fore{r}",
+        )(*ins)
 
     def back_call(r, grads, pick, scale, before):
         def kernel(*refs):
@@ -298,7 +313,7 @@
             name=f"back{r}",
         )(*ins)
 
-    def act_call(r, fore, back, pick, scale, before):
+    def act_call(r, me_arr, fore, back, pick, scale, before):
         tile = step_cols
 
         def kernel(*refs):
@@ -330,31 +345,14 @@
     meta = jnp.pad(meta, ((0, 0), (0, LANES - meta.shape[1])))
     tokens = jnp.concatenate([tokens_in, meta], axis=1)
 
-    rest = near[1:]
-    turn = rest[::-1] + [0]
-    fore, back, pick, scale, sums, lines_of = {}, {}, {}, {}, {}, {}
+    far = near[1:]
+    turn = far + [0]
+    fore, back, pick, scale = {}, {}, {}, {}
+    dense, line, total, sums = {}, {}, {}, {}
     hold = {"fore": None, "back": None, "act": None}
-    y_done = []
-
-    def done(kind):
-        return hold[kind][0]
-
-    def run_lines(r, block, after):
-        lines = [block]
-        for i in range(1, n_in):
-            x = gate(block, (*after, *y_done[-1:]))
-            y_done.append(shift(x, 1, i, f"tok{r}_y"))
-            lines.append(y_done[-1])
-        return lines
-
-    def run_fore(r, lines, *after):
-        blocks = []
-        for line in lines:
-            blocks.append(line)
-            for c in range(1, n_core):
-                blocks.append(shift(line, 2, c, f"tok{r}_core"))
-        blocks[0] = gate(blocks[0], after)
-        rows_in, part, pick[r], scale[r] = fore_call(r, blocks, hold["fore"])
+
+    def run_fore(r, blocks, places):
+        rows_in, part, pick[r], scale[r] = fore_call(r, blocks, places, hold["fore"])
         hold["fore"] = [rows_in]
         fore[r] = exchange(part, f"fore{r}")
 
@@ -363,53 +361,66 @@
         hold["back"] = [rows_back]
         back[r] = exchange(part, f"back{r}")
 
-    def run_act(r, *after):
+    def run_act(r, me_now, *after):
         came = [gate(back[r][0], after), *back[r][1:]]
-        hidden, dgate, dup, *dense = act_call(r, fore[r], came, pick[r], scale[r], hold["act"])
-        hold["act"] = [hidden, dgate, dup]
-        came = [shift(dense[c], 2, -c, f"sum{r}_core") for c in range(1, n_core)]
-        lines_of[r] = [
-            sum([x[i].astype(F32) for x in came], dense[0][i].astype(F32)).astype(BF16)
+        out = act_call(r, me_now, fore[r], came, pick[r], scale[r], hold["act"])
+        hold["act"], dense[r] = out[:3], out[3:]
+
+    def sum_core(r, *after):
+        came = [shift(gate(dense[r][c], after), 2, -c, f"sum{r}_core") for c in range(1, n_core)]
+        line[r] = [
+            sum([x[i].astype(F32) for x in came], dense[r][0][i].astype(F32)).astype(BF16)
             for i in range(n_in)
         ]
 
-    def run_sum(r, acted, came, before):
-        after = tuple(x for x in (came, before) if x is not None)
-        total = gate(lines_of[r][0], acted).astype(F32)
+    def sum_in(r, *after):
+        held = gate(line[r][0], after).astype(F32)
         for i in range(1, n_in):
-            total = total + shift(gate(lines_of[r][i], after), 1, -i, f"sum{r}_y").astype(F32)
-        sums[r] = total = total.astype(BF16)
+            held = held + shift(line[r][i], 1, -i, f"sum{r}_y").astype(F32)
+        total[r] = held.astype(BF16)
+        pieces = [total[r]]
+        if min(r, n_out - r) >= 2:
+            half = LANES * ((width + extra) // LANES // 2)
+            pieces = [total[r][:, half:], total[r][:, :half]]
         if r:
-            sums[r] = shift(total, 0, -r, f"sum{r}_z")
-        return total
-
-    block = {0: tokens}
-    for k, r in enumerate(rest):
-        block[r] = shift(gate(tokens, block[rest[k - 2]] if k >= 2 else None), 0, r, f"tok{r}_z")
-    grads = lax.all_gather(gate(out_grad, None), "dp", axis=0)
-    lines = {0: run_lines(0, tokens, ())}
-    for k, r in enumerate(near):
-        if k + 1 < n_out:
-            lines[near[k + 1]] = run_lines(near[k + 1], block[near[k + 1]], ())
-        run_fore(r, lines[r])
-        before = (done("fore"), *([fore[near[k - 1]][-1]] if k else []))
-        if k + 1 < n_out:
-            nxt = near[k + 1]
-            lines[nxt] = [gate(line, before) for line in lines[nxt]]
-        if k + 2 < n_out:
-            nxt = near[k + 2]
-            block[nxt] = gate(block[nxt], done("fore"))
+            pieces = [shift(x, 0, -r, f"sum{r}_z") for x in pieces]
+        sums[r] = pieces
+
+    tokens_all = lax.all_gather(tokens, "dp", axis=0)
+    grads = lax.all_gather(gate(out_grad, tokens_all), "dp", axis=0)
+    for r in turn:
+        places = [source(r, i, c) for i in range(n_in) for c in range(n_core)]
+        run_fore(r, [tokens_all] * members, places)
+    run_back(turn[0], hold["fore"][0], *[fore[r][-1] for r in turn[:-1]])
+    for r in turn[1:3]:
+        run_back(r)
+    first = back[turn[0]][-1]
+    there = shift(gate(me_arr, (first, hold["back"][0])), 2, 1, "tick")
+    me_now = there - (place[2] + 1) % n_core + place[2]
     for k, r in enumerate(turn):
-        run_back(r, done("fore"), *([fore[near[-1]][-1]] if k else [fore[near[-2]][-1]]))
-    total = None
-    for k, r in enumerate(turn):
-        run_act(r, done("back"), *([] if k == 0 else [lines_of[turn[k - 1]][-1]]))
+        run_act(r, me_now, *([line[turn[k - 1]][0]] if k else []))
         if k:
-            total = run_sum(turn[k - 1], done("act"), back[r][-1], total)
-    run_sum(turn[-1], None, None, total)
+            sum_in(turn[k - 1], dense[r][0])
+        if 3 <= k + 2 < n_out:
+            run_back(turn[k + 2], dense[r][0])
+        after = [back[turn[k + 1]][-1]] if k + 1 < n_out else []
+        if k >= 1:
+            after.append(total[turn[k - 1]])
+        if k >= 2:
+            after.append(sums[turn[0]][min(k - 2, len(sums[turn[0]]) - 1)])
+        if k == min(0, n_out - 2):
+            after.append(fore[turn[-1]][-1])
+        sum_core(r, *after)
+    sum_in(turn[-1])
+    full = sum(jnp.concatenate(sums[r][::-1], axis=1).astype(F32) for r in near)
+    input_grad = full[:, :width].astype(BF16)
+    dots_of = full[:, width : width + total_experts]
+    named = expert_ids[:, :, None] == jnp.arange(total_experts, dtype=jnp.int32)[None, None, :]
+    weight_grad = jnp.sum(jnp.where(named, dots_of[:, None, :], 0.0), axis=2).astype(BF16)
+
     rows_in, rows_back = hold["fore"][0], hold["back"][0]
     hidden, dgate, dup = hold["act"]
-    full = sum(sums[r].astype(F32) for r in near)
+    full = sum(jnp.concatenate(sums[r][::-1], axis=1).astype(F32) for r in near)
     input_grad = full[:, :width].astype(BF16)
     dots_of = full[:, width : width + total_experts]
     named = expert_ids[:, :, None] == jnp.arange(total_experts, dtype=jnp.int32)[None, None, :]

time: 464 us -> 452 us (0.974)
  starting transfers between devices: 60.7 us -> 31.4 us
  Pallas kernels: 129 us -> 135 us
  waiting for transfers between devices: 194 us -> 200 us
    all_gather x1 -> x2, waiting for transfers between devices: 0.01 us -> 127 us  [the longest x1 116 us: body(): tokens_all = lax.all_gather(tokens, 'dp', axis=0)]
    ppermute x26 -> x13, waiting for transfers between devices: 138 us -> 30.3 us  [shift(): return lax.ppermute(x, 'dp', pairs)]
    pallas_call x0 -> x4, Pallas kernels: none -> 50.7 us  [fore_call(): pl.pallas_call(kernel, grid_spec=pltpu.PrefetchScalarGridSpec(num_scalar_...]
    pallas_call x8 -> x4, Pallas kernels: 97 us -> 52.5 us  [call(): pl.pallas_call(kernel, grid=(grid,), in_specs=in_specs, out_specs=out_spe...]
    ppermute x26 -> x13, starting transfers between devices: 51.9 us -> 24.9 us  [shift(): return lax.ppermute(x, 'dp', pairs)]
    ppermute x8, waiting for transfers between devices: 55.7 us -> 43.1 us  [exchange(): parts.append(lax.ppermute(part, 'expert', pairs))]
    unnamed x52 -> x55, local copies, waits for them, and re-layouts: 10.8 us -> 14.1 us
  transfers between devices with their start and end apart: 35 -> 23, of which waited for: 17 -> 10; matrix products, arithmetic and copies ran while one was open for 10% -> 10% of each run, Pallas kernels for 25% -> 30%
where the time goes in v2:
time: 452 us; the launch traced here: 449 us
  waiting for transfers between devices  200 us (44%)
  Pallas kernels  135 us (30%)
  matrix products  37.3 us (8%)
  starting transfers between devices  31.4 us (7%)
  other arithmetic  15.4 us (3%)
  local copies, waits for them, and re-layouts  15.2 us (3%)
  between operations  15 us (3%)
    all_gather x1, waiting for transfers between devices, body(): tokens_all = lax.all_gather(tokens, 'dp', axis=0)  116 us
    pallas_call x4, Pallas kernels, call(): pl.pallas_call(kernel, grid=(grid,), in_specs=in_specs, out_specs=out_spe...  52.5 us
    pallas_call x4, Pallas kernels, fore_call(): pl.pallas_call(kernel, grid_spec=pltpu.PrefetchScalarGridSpec(num_scalar_...  50.7 us
    ppermute x8, waiting for transfers between devices, exchange(): parts.append(lax.ppermute(part, 'expert', pairs))  43.1 us
    dot_general x3, matrix products, dot(): return lax.dot_general(a, b, (dims, ((), ())), preferred_element_type=F32)  37.3 us
    pallas_call x4, Pallas kernels, back_call(): pl.pallas_call(kernel, grid_spec=pltpu.PrefetchScalarGridSpec(num_scalar_...  31.6 us
    ppermute x13, waiting for transfers between devices, shift(): return lax.ppermute(x, 'dp', pairs)  30.3 us
    ppermute x13, starting transfers between devices, shift(): return lax.ppermute(x, 'dp', pairs)  24.9 us
  transfers between devices with their start and end apart: 23, of which 10 were waited for; matrix products, arithmetic and copies ran while one was open for 10% of the time, Pallas kernels for 30%

profile of v2, /device:TPU:13, one launch (start us, length us, event | category | flops | bytes accessed | tf_op | source)
XLA Modules:
  0.0 449.3 jit_solution(13091812799460219580)
XLA Ops:
  8.7 2.2 fusion.5
  11.0 116.1 %all-gather.5.cloned.1.call-done = bf16[2048,3712]{1,0:T(8,128)(2,1)} async-done(((bf16[128,3712]{1,0:T(8,128)(2,1)}), bf16[2048,3712]{1,0:T(8,128)(2,1)}) %all-gather.5.cloned.1.call-update) | async-done | bytes 15204368 | tf_op jit(solution)/shard_map/all_gather | solution.py:389
  127.4 3.1 copy-done
  130.5 12.9 %fore2.1 = (bf16[1280,3584]{1,0:T(8,128)(2,1)}, bf16[2,320,1024]{2,1,0:T(8,128)(2,1)}, bf16[4,128,128]{2,1,0:T(8,128)(2,1)S(1)}, f32[320,128]{1,0:T(8,128)S(1)}) custom-call(s32[4]{0:T(128)S(1)} %pad_add_fusion.refs_0_, s32[1]{0:T(128)} %bitcast.refs_1_, bf16[16,128,3712]{2,1,0:T(8,128)(2,1)} %bitcast.56, bf16[16,128,3712]{2,1,0:T(8,128)(2,1)} %bitcast.57, ...), custom_call_target="tpu_custom_call" | custom-call | flops 4697620 | tf_op jit(solution)/shard_map/fore2/pallas_call | solution.py:252
  144.1 1.2 collective-permute-start
  145.3 12.5 %fore1.1 = (bf16[1280,3584]{1,0:T(8,128)(2,1)}, bf16[2,320,1024]{2,1,0:T(8,128)(2,1)}, bf16[4,128,128]{2,1,0:T(8,128)(2,1)S(1)}, f32[320,128]{1,0:T(8,128)S(1)}) custom-call(s32[4]{0:T(128)S(1)} %pad_add_fusion.3.refs_0_, s32[1]{0:T(128)} %bitcast.refs_1_, bf16[16,128,3712]{2,1,0:T(8,128)(2,1)} %bitcast.60, ...), custom_call_target="tpu_custom_call", output_to_operand_aliasing={{0}: (8, {})} | custom-call | flops 4697620 | tf_op jit(solution)/shard_map/fore1/pallas_call | solution.py:252
  158.0 12.3 %fore3.1 = (bf16[1280,3584]{1,0:T(8,128)(2,1)}, bf16[2,320,1024]{2,1,0:T(8,128)(2,1)S(1)}, bf16[4,128,128]{2,1,0:T(8,128)(2,1)S(1)}, f32[320,128]{1,0:T(8,128)S(1)}) custom-call(s32[4]{0:T(128)S(1)} %pad_add_fusion.2.refs_0_, s32[1]{0:T(128)} %bitcast.refs_1_, bf16[16,128,3712]{2,1,0:T(8,128)(2,1)} %bitcast.64, ...), custom_call_target="tpu_custom_call", output_to_operand_aliasing={{0}: (8, {})} | custom-call | flops 4697620 | tf_op jit(solution)/shard_map/fore3/pallas_call | solution.py:252
  170.3 1.2 collective-permute-start.2
  171.6 3.1 copy-done.2
  174.7 13.0 %fore0.1 = (bf16[1280,3584]{1,0:T(8,128)(2,1)}, bf16[2,320,1024]{2,1,0:T(8,128)(2,1)S(1)}, bf16[4,128,128]{2,1,0:T(8,128)(2,1)S(1)}, f32[320,128]{1,0:T(8,128)S(1)}) custom-call(s32[4]{0:T(128)S(1)} %pad_add_fusion.1.refs_0_, s32[1]{0:T(128)} %bitcast.refs_1_, bf16[16,128,3712]{2,1,0:T(8,128)(2,1)} %bitcast.68, ...), custom_call_target="tpu_custom_call", output_to_operand_aliasing={{0}: (8, {})} | custom-call | flops 4697620 | tf_op jit(solution)/shard_map/fore0/pallas_call | solution.py:252
  187.7 15.0 %collective-permute-done.1.refs_2_ = bf16[2,320,1024]{2,1,0:T(8,128)(2,1)} collective-permute-done((bf16[2,320,1024]{2,1,0:T(8,128)(2,1)}, bf16[2,320,1024]{2,1,0:T(8,128)(2,1)}, u32[]{:S(2)}, u32[]{:S(2)}) %collective-permute-start.1) | collective-permute-done | bytes 1310752 | tf_op jit(solution)/shard_map/fore1_x/ppermute | solution.py:201
  202.7 28.1 %collective-permute-done.2.refs_2_ = bf16[2,320,1024]{2,1,0:T(8,128)(2,1)} collective-permute-done((bf16[2,320,1024]{2,1,0:T(8,128)(2,1)S(1)}, bf16[2,320,1024]{2,1,0:T(8,128)(2,1)}, u32[]{:S(2)}, u32[]{:S(2)}) %collective-permute-start.2) | collective-permute-done | bytes 1310752 | tf_op jit(solution)/shard_map/fore3_x/ppermute | solution.py:201
  230.8 10.7 %all-gather.7.cloned.1.call-done = bf16[2048,3584]{1,0:T(8,128)(2,1)} async-done(((bf16[128,3584]{1,0:T(8,128)(2,1)}), bf16[2048,3584]{1,0:T(8,128)(2,1)}) %all-gather.7.cloned.1.call-update) | async-done | bytes 14680080 | tf_op jit(solution)/shard_map/all_gather | solution.py:390
  241.5 3.1 copy-done.3
  245.5 7.8 %back2.1 = (bf16[1280,3584]{1,0:T(8,128)(2,1)}, bf16[320,1024]{1,0:T(8,128)(2,1)}) custom-call(s32[4]{0:T(128)S(1)} %pad_add_fusion.refs_0_, bf16[16,128,3584]{2,1,0:T(8,128)(2,1)} %bitcast.72, bf16[16,128,3584]{2,1,0:T(8,128)(2,1)} %bitcast.73, bf16[16,128,3584]{2,1,0:T(8,128)(2,1)} %bitcast.74, bf16[16,128,3584]{2,1,0:T(8,128)(2,1)} %bitcast.75, ...), custom_call_target="tpu_custom_call" | custom-call | flops 2348810 | tf_op jit(solution)/shard_map/back2/pallas_call | solution.py:297
  253.3 1.2 collective-permute-start.3
  254.5 8.1 %back1.1 = (bf16[1280,3584]{1,0:T(8,128)(2,1)}, bf16[320,1024]{1,0:T(8,128)(2,1)}) custom-call(s32[4]{0:T(128)S(1)} %pad_add_fusion.3.refs_0_, bf16[16,128,3584]{2,1,0:T(8,128)(2,1)} %bitcast.76, bf16[16,128,3584]{2,1,0:T(8,128)(2,1)} %bitcast.77, bf16[16,128,3584]{2,1,0:T(8,128)(2,1)} %bitcast.78, ...), custom_call_target="tpu_custom_call", output_to_operand_aliasing={{0}: (8, {})} | custom-call | flops 2348810 | tf_op jit(solution)/shard_map/back1/pallas_call | solution.py:297
  262.8 3.1 copy-done.4
  265.9 7.9 %back3.1 = (bf16[1280,3584]{1,0:T(8,128)(2,1)}, bf16[320,1024]{1,0:T(8,128)(2,1)S(1)}) custom-call(s32[4]{0:T(128)S(1)} %pad_add_fusion.2.refs_0_, bf16[16,128,3584]{2,1,0:T(8,128)(2,1)} %bitcast.80, bf16[16,128,3584]{2,1,0:T(8,128)(2,1)} %bitcast.81, bf16[16,128,3584]{2,1,0:T(8,128)(2,1)} %bitcast.82, ...), custom_call_target="tpu_custom_call", output_to_operand_aliasing={{0}: (8, {})} | custom-call | flops 2348810 | tf_op jit(solution)/shard_map/back3/pallas_call | solution.py:297
  273.8 1.6 collective-permute-start.4
  276.1 13.3 %act2.1 = (bf16[1280,1024]{1,0:T(8,128)(2,1)}, bf16[1280,1024]{1,0:T(8,128)(2,1)}, bf16[1280,1024]{1,0:T(8,128)(2,1)}, bf16[2,128,3712]{2,1,0:T(8,128)(2,1)S(1)}, bf16[2,128,3712]{2,1,0:T(8,128)(2,1)S(1)}) custom-call(s32[1]{0:T(128)S(6)} %add.401.refs_0_, bf16[2,320,1024]{2,1,0:T(8,128)(2,1)} %get-tuple-element.68.refs_1_, ...), custom_call_target="tpu_custom_call" | custom-call | flops 4697620 | tf_op jit(solution)/shard_map/act2/pallas_call | solution.py:217
  289.8 3.6 collective-permute-done.7
  293.4 1.4 fusion.7
  294.8 1.2 collective-permute-start.9
  295.9 1.2 collective-permute-start.8
  297.1 13.5 %act1.1 = (bf16[1280,1024]{1,0:T(8,128)(2,1)}, bf16[1280,1024]{1,0:T(8,128)(2,1)}, bf16[1280,1024]{1,0:T(8,128)(2,1)}, bf16[2,128,3712]{2,1,0:T(8,128)(2,1)S(1)}, bf16[2,128,3712]{2,1,0:T(8,128)(2,1)S(1)}) custom-call(s32[1]{0:T(128)S(6)} %add.401.refs_0_, ...), custom_call_target="tpu_custom_call", output_to_operand_aliasing={{0}: (9, {}), {1}: (10, {}), {2}: (11, {})} | custom-call | flops 4697620 | tf_op jit(solution)/shard_map/act1/pallas_call | solution.py:217
  310.6 6.8 %collective-permute-done.9 = bf16[128,3712]{1,0:T(8,128)(2,1)} collective-permute-done((bf16[128,3712]{1,0:T(8,128)(2,1)}, bf16[128,3712]{1,0:T(8,128)(2,1)}, u32[]{:S(2)}, u32[]{:S(2)}) %collective-permute-start.9) | collective-permute-done | bytes 950304 | tf_op jit(solution)/shard_map/sum2_y/ppermute | solution.py:187
  317.4 1.4 add_convert_fusion.8
  320.0 3.5 collective-permute-done.10
  324.0 1.3 collective-permute-start.12
  325.3 7.8 %back0.1 = (bf16[1280,3584]{1,0:T(8,128)(2,1)}, bf16[320,1024]{1,0:T(8,128)(2,1)S(1)}) custom-call(s32[4]{0:T(128)S(1)} %pad_add_fusion.1.refs_0_, bf16[16,128,3584]{2,1,0:T(8,128)(2,1)} %bitcast.84, bf16[16,128,3584]{2,1,0:T(8,128)(2,1)} %bitcast.85, bf16[16,128,3584]{2,1,0:T(8,128)(2,1)} %bitcast.86, ...), custom_call_target="tpu_custom_call", output_to_operand_aliasing={{0}: (8, {})} | custom-call | flops 2348810 | tf_op jit(solution)/shard_map/back0/pallas_call | solution.py:297
  333.1 1.2 collective-permute-start.11
  334.3 1.9 collective-permute-start.13
  336.2 12.9 %act3.1 = (bf16[1280,1024]{1,0:T(8,128)(2,1)}, bf16[1280,1024]{1,0:T(8,128)(2,1)}, bf16[1280,1024]{1,0:T(8,128)(2,1)}, bf16[2,128,3712]{2,1,0:T(8,128)(2,1)S(1)}, bf16[2,128,3712]{2,1,0:T(8,128)(2,1)S(1)}) custom-call(s32[1]{0:T(128)S(6)} %add.401.refs_0_, ...), custom_call_target="tpu_custom_call", output_to_operand_aliasing={{0}: (9, {}), {1}: (10, {}), {2}: (11, {})} | custom-call | flops 4697620 | tf_op jit(solution)/shard_map/act3/pallas_call | solution.py:217
  349.1 1.2 add_convert_fusion.5
  350.3 6.3 %collective-permute-done.13 = bf16[128,1920]{1,0:T(8,128)(2,1)S(1)} collective-permute-done((bf16[128,1920]{1,0:T(8,128)(2,1)S(1)}, bf16[128,1920]{1,0:T(8,128)(2,1)S(1)}, u32[]{:S(2)}, u32[]{:S(2)}) %collective-permute-start.13) | collective-permute-done | bytes 491552 | tf_op jit(solution)/shard_map/sum2_z/ppermute | solution.py:187
  356.6 1.6 collective-permute-start.14
  358.2 3.2 collective-permute-start.16
  361.9 1.7 fusion.10
  363.9 12.8 %act0.1 = (bf16[1280,1024]{1,0:T(8,128)(2,1)}, bf16[1280,1024]{1,0:T(8,128)(2,1)}, bf16[1280,1024]{1,0:T(8,128)(2,1)}, bf16[2,128,3712]{2,1,0:T(8,128)(2,1)S(1)}, bf16[2,128,3712]{2,1,0:T(8,128)(2,1)S(1)}) custom-call(s32[1]{0:T(128)S(6)} %add.401.refs_0_, ...), custom_call_target="tpu_custom_call", output_to_operand_aliasing={{0}: (9, {}), {1}: (10, {}), {2}: (11, {})} | custom-call | flops 4697620 | tf_op jit(solution)/shard_map/act0/pallas_call | solution.py:217
  376.7 13.6 %fusion.1 = bf16[1,3584,1024]{2,1,0:T(8,128)(2,1)} fusion(bf16[1280,3584]{1,0:T(8,128)(2,1)S(1)} %bitcast.89, bf16[1280,1024]{1,0:T(8,128)(2,1)} %get-tuple-element.117), kind=kOutput, calls=%fused_computation.4 | convolution fusion | flops 9398910976 | bytes 19136512 | tf_op jit(solution)/shard_map/dot_general | solution.py:34
  390.3 2.5 add_convert_fusion.2
  393.7 11.8 %fusion.2 = bf16[1,3584,1024]{2,1,0:T(8,128)(2,1)} fusion(bf16[1280,3584]{1,0:T(8,128)(2,1)S(1)} %bitcast.89, bf16[1280,1024]{1,0:T(8,128)(2,1)S(1)} %copy-done.14), kind=kOutput, calls=%fused_computation.5 | convolution fusion | flops 9398910976 | bytes 19136512 | tf_op jit(solution)/shard_map/dot_general | solution.py:34
  405.4 10.7 %collective-permute-start.20 = (bf16[128,3712]{1,0:T(8,128)(2,1)}, bf16[128,3712]{1,0:T(8,128)(2,1)S(1)}, u32[]{:S(2)}, u32[]{:S(2)}) collective-permute-start(bf16[128,3712]{1,0:T(8,128)(2,1)} %add_convert_fusion.2), channel_id=1, source_target_pairs={{4,0},{5,1},{6,2},{7,3},{8,4},{9,5},{10,6},{11,7},{12,8},{13,9},{1... | collective-permute-start | bytes 2850824 | tf_op jit(solution)/shard_map/sum3_z/ppermute | solution.py:187
  416.7 11.9 %fusion = bf16[1,1024,3584]{2,1,0:T(8,128)(2,1)} fusion(bf16[1280,1024]{1,0:T(8,128)(2,1)S(1)} %copy-done.13, bf16[1280,3584]{1,0:T(8,128)(2,1)S(1)} %bitcast.91), kind=kOutput, calls=%fused_computation.3 | convolution fusion | flops 9398910976 | bytes 19136512 | tf_op jit(solution)/shard_map/dot_general | solution.py:34
  428.6 8.2 %collective-permute-done.20 = bf16[128,3712]{1,0:T(8,128)(2,1)S(1)} collective-permute-done((bf16[128,3712]{1,0:T(8,128)(2,1)}, bf16[128,3712]{1,0:T(8,128)(2,1)S(1)}, u32[]{:S(2)}, u32[]{:S(2)}) %collective-permute-start.20) | collective-permute-done | bytes 950304 | tf_op jit(solution)/shard_map/sum3_z/ppermute | solution.py:187
  436.8 1.9 collective-permute-done.18
  438.7 2.0 convert_add_fusion.1
  (94 shorter events, 10.1 us)
Async XLA Ops:
  7.2 119.9 %all-gather.5.cloned.1.call-start = ((), (), s32[]{:S(2)}) async-start(), calls=%async_computation | async-start | bytes 16154624 | tf_op jit(solution)/shard_map/all_gather | solution.py:389
  10.9 230.5 %all-gather.7.cloned.1.call-start = ((), (), s32[]{:S(2)}) async-start(), calls=%async_computation.1 | async-start | bytes 15597568 | tf_op jit(solution)/shard_map/all_gather | solution.py:390
  127.4 3.1 copy-start
  130.5 14.8 %copy-start.1 = (bf16[1,3584,1024]{2,1,0:T(8,128)(2,1)S(1)}, bf16[1,3584,1024]{2,1,0:T(8,128)(2,1)}, u32[]{:S(2)}) copy-start(bf16[1,3584,1024]{2,1,0:T(8,128)(2,1)} %refs_7_.23) | copy-start | bytes 22020100
  144.1 43.6 %collective-permute-start = (bf16[2,320,1024]{2,1,0:T(8,128)(2,1)}, bf16[2,320,1024]{2,1,0:T(8,128)(2,1)}, u32[]{:S(2)}, u32[]{:S(2)}) collective-permute-start(bf16[2,320,1024]{2,1,0:T(8,128)(2,1)} %get-tuple-element.68.refs_1_), channel_id=1, source_target_pairs={{16,0},{0,16},{17,1},{1,17},{18,2},{2,18},{19,3},{3,19},{20,4},{4,... | collective-permute-start | bytes 3932168 | tf_op jit(solution)/shard_map/fore2_x/ppermute | solution.py:201
  157.8 12.5 %copy-start.7 = (bf16[4,128,128]{2,1,0:T(8,128)(2,1)}, bf16[4,128,128]{2,1,0:T(8,128)(2,1)S(1)}, u32[]{:S(2)}) copy-start(bf16[4,128,128]{2,1,0:T(8,128)(2,1)S(1)} %get-tuple-element.77.refs_5_) | copy-start | bytes 393220
  157.8 44.9 %collective-permute-start.1 = (bf16[2,320,1024]{2,1,0:T(8,128)(2,1)}, bf16[2,320,1024]{2,1,0:T(8,128)(2,1)}, u32[]{:S(2)}, u32[]{:S(2)}) collective-permute-start(bf16[2,320,1024]{2,1,0:T(8,128)(2,1)} %get-tuple-element.69.refs_1_), channel_id=1, source_target_pairs={{16,0},{0,16},{17,1},{1,17},{18,2},{2,18},{19,3},{3,19},{20,4},{4,... | collective-permute-start | bytes 3932168 | tf_op jit(solution)/shard_map/fore1_x/ppermute | solution.py:201
  170.3 60.5 %collective-permute-start.2 = (bf16[2,320,1024]{2,1,0:T(8,128)(2,1)S(1)}, bf16[2,320,1024]{2,1,0:T(8,128)(2,1)}, u32[]{:S(2)}, u32[]{:S(2)}) collective-permute-start(bf16[2,320,1024]{2,1,0:T(8,128)(2,1)S(1)} %get-tuple-element.70.refs_1_), channel_id=1, source_target_pairs={{16,0},{0,16},{17,1},{1,17},{18,2},{2,18},{19,3},{3,19},{20,4},{4,... | collective-permute-start | bytes 3932168 | tf_op jit(solution)/shard_map/fore3_x/ppermute | solution.py:201
  171.6 3.1 copy-start.2
  187.7 101.7 %collective-permute-start.5 = (bf16[2,320,1024]{2,1,0:T(8,128)(2,1)S(1)}, bf16[2,320,1024]{2,1,0:T(8,128)(2,1)}, u32[]{:S(2)}, u32[]{:S(2)}) collective-permute-start(bf16[2,320,1024]{2,1,0:T(8,128)(2,1)S(1)} %get-tuple-element.83.refs_1_), channel_id=1, source_target_pairs={{16,0},{0,16},{17,1},{1,17},{18,2},{2,18},{19,3},{3,19},{20,4},{4,... | collective-permute-start | bytes 3932168 | tf_op jit(solution)/shard_map/fore0_x/ppermute | solution.py:201
  241.5 3.1 copy-start.3
  245.5 9.0 %copy-start.8 = (bf16[4,128,128]{2,1,0:T(8,128)(2,1)S(1)}, bf16[4,128,128]{2,1,0:T(8,128)(2,1)}, u32[]{:S(2)}) copy-start(bf16[4,128,128]{2,1,0:T(8,128)(2,1)} %copy-done.7) | copy-start | bytes 393220
  253.3 20.5 %collective-permute-start.3 = (bf16[320,1024]{1,0:T(8,128)(2,1)}, bf16[320,1024]{1,0:T(8,128)(2,1)}, u32[]{:S(2)}, u32[]{:S(2)}) collective-permute-start(bf16[320,1024]{1,0:T(8,128)(2,1)} %get-tuple-element.74.refs_3_), channel_id=1, source_target_pairs={{16,0},{0,16},{17,1},{1,17},{18,2},{2,18},{19,3},{3,19},{20,4},{4,... | collective-permute-start | bytes 1966088 | tf_op jit(solution)/shard_map/back2_x/ppermute | solution.py:201
  262.6 26.9 %collective-permute-start.6 = (bf16[320,1024]{1,0:T(8,128)(2,1)}, bf16[320,1024]{1,0:T(8,128)(2,1)}, u32[]{:S(2)}, u32[]{:S(2)}) collective-permute-start(bf16[320,1024]{1,0:T(8,128)(2,1)} %get-tuple-element.88.refs_3_), channel_id=1, source_target_pairs={{16,0},{0,16},{17,1},{1,17},{18,2},{2,18},{19,3},{3,19},{20,4},{4,... | collective-permute-start | bytes 1966088 | tf_op jit(solution)/shard_map/back1_x/ppermute | solution.py:201
  262.8 3.1 copy-start.4
  265.9 10.2 %copy-start.12 = (bf16[4,128,128]{2,1,0:T(8,128)(2,1)S(1)}, bf16[4,128,128]{2,1,0:T(8,128)(2,1)}, u32[]{:S(2)}) copy-start(bf16[4,128,128]{2,1,0:T(8,128)(2,1)} %copy-done.10) | copy-start | bytes 393220
  273.8 1.6 collective-permute-start.4
  289.4 3.9 collective-permute-start.7
  293.4 3.7 copy-start.9
  294.8 22.7 %collective-permute-start.9 = (bf16[128,3712]{1,0:T(8,128)(2,1)}, bf16[128,3712]{1,0:T(8,128)(2,1)}, u32[]{:S(2)}, u32[]{:S(2)}) collective-permute-start(bf16[128,3712]{1,0:T(8,128)(2,1)} %get-tuple-element.125), channel_id=1, source_target_pairs={{2,0},{3,1},{0,2},{1,3},{6,4},{7,5},{4,6},{5,7},{10,8},{11,9},{8,1... | collective-permute-start | bytes 2850824 | tf_op jit(solution)/shard_map/sum2_y/ppermute | solution.py:187
  295.9 22.9 %collective-permute-start.8 = (bf16[320,1024]{1,0:T(8,128)(2,1)S(1)}, bf16[320,1024]{1,0:T(8,128)(2,1)S(1)}, u32[]{:S(2)}, u32[]{:S(2)}) collective-permute-start(bf16[320,1024]{1,0:T(8,128)(2,1)S(1)} %get-tuple-element.101.refs_3_), channel_id=1, source_target_pairs={{16,0},{0,16},{17,1},{1,17},{18,2},{2,18},{19,3},{3,19},{20,4},{4,... | collective-permute-start | bytes 1966088 | tf_op jit(solution)/shard_map/back3_x/ppermute | solution.py:201
  297.1 28.1 %slice-start = ((s8[7340032]{0:T(1024)(128)(4,1)}), s8[4194304]{0:T(1024)(128)(4,1)S(1)}, s32[]{:S(2)}) async-start(s8[7340032]{0:T(1024)(128)(4,1)} %bitcast.54), calls=%async_computation.2 | async-start | bytes 8388608
  297.1 28.1 %slice-start.1 = ((s8[7340032]{0:T(1024)(128)(4,1)}), s8[3145728]{0:T(1024)(128)(4,1)S(1)}, s32[]{:S(2)}) async-start(s8[7340032]{0:T(1024)(128)(4,1)} %bitcast.54), calls=%async_computation.3 | async-start | bytes 6291456
  318.9 5.1 %copy-start.5 = (bf16[320,1024]{1,0:T(8,128)(2,1)}, bf16[320,1024]{1,0:T(8,128)(2,1)S(1)}, u32[]{:S(2)}) copy-start(bf16[320,1024]{1,0:T(8,128)(2,1)S(1)} %collective-permute-done.8.refs_4_) | copy-start | bytes 1966084
  318.9 4.7 %collective-permute-start.10 = (bf16[2,128,3712]{2,1,0:T(8,128)(2,1)S(1)}, bf16[2,128,3712]{2,1,0:T(8,128)(2,1)S(1)}, u32[]{:S(2)}, u32[]{:S(2)}) collective-permute-start(bf16[2,128,3712]{2,1,0:T(8,128)(2,1)S(1)} %get-tuple-element.100), channel_id=1, source_target_pairs={{1,0},{0,1},{3,2},{2,3},{5,4},{4,5},{7,6},{6,7},{9,8},{8,9},{11,10... | collective-permute-start | bytes 5701640 | tf_op jit(solution)/shard_map/sum1_core/ppermute | solution.py:187
  324.0 25.1 %collective-permute-start.12 = (bf16[128,3712]{1,0:T(8,128)(2,1)S(1)}, bf16[128,3712]{1,0:T(8,128)(2,1)S(1)}, u32[]{:S(2)}, u32[]{:S(2)}) collective-permute-start(bf16[128,3712]{1,0:T(8,128)(2,1)S(1)} %get-tuple-element.123), channel_id=1, source_target_pairs={{2,0},{3,1},{0,2},{1,3},{6,4},{7,5},{4,6},{5,7},{10,8},{11,9},{8,1... | collective-permute-start | bytes 2850824 | tf_op jit(solution)/shard_map/sum1_y/ppermute | solution.py:187
  325.2 11.0 %copy-start.6 = (bf16[320,1024]{1,0:T(8,128)(2,1)S(1)}, bf16[320,1024]{1,0:T(8,128)(2,1)}, u32[]{:S(2)}) copy-start(bf16[320,1024]{1,0:T(8,128)(2,1)} %copy-done.5) | copy-start | bytes 1966084
  333.1 17.2 %collective-permute-start.11 = (bf16[320,1024]{1,0:T(8,128)(2,1)S(1)}, bf16[320,1024]{1,0:T(8,128)(2,1)S(1)}, u32[]{:S(2)}, u32[]{:S(2)}) collective-permute-start(bf16[320,1024]{1,0:T(8,128)(2,1)S(1)} %get-tuple-element.109.refs_3_), channel_id=1, source_target_pairs={{16,0},{0,16},{17,1},{1,17},{18,2},{2,18},{19,3},{3,19},{20,4},{4,... | collective-permute-start | bytes 1966088 | tf_op jit(solution)/shard_map/back0_x/ppermute | solution.py:201
  334.3 22.3 %collective-permute-start.13 = (bf16[128,1920]{1,0:T(8,128)(2,1)S(1)}, bf16[128,1920]{1,0:T(8,128)(2,1)S(1)}, u32[]{:S(2)}, u32[]{:S(2)}) collective-permute-start(bf16[128,1920]{1,0:T(8,128)(2,1)S(1)} %slice.85), channel_id=1, source_target_pairs={{8,0},{9,1},{10,2},{11,3},{12,4},{13,5},{14,6},{15,7},{0,8},{1,9},... | collective-permute-start | bytes 1474568 | tf_op jit(solution)/shard_map/sum2_z/ppermute | solution.py:187
  356.6 7.0 %copy-start.16 = (bf16[128,1920]{1,0:T(8,128)(2,1)}, bf16[128,1920]{1,0:T(8,128)(2,1)S(1)}, u32[]{:S(2)}) copy-start(bf16[128,1920]{1,0:T(8,128)(2,1)S(1)} %collective-permute-done.13) | copy-start | bytes 1474564
  356.6 5.3 %collective-permute-start.14 = (bf16[2,128,3712]{2,1,0:T(8,128)(2,1)S(1)}, bf16[2,128,3712]{2,1,0:T(8,128)(2,1)S(1)}, u32[]{:S(2)}, u32[]{:S(2)}) collective-permute-start(bf16[2,128,3712]{2,1,0:T(8,128)(2,1)S(1)} %get-tuple-element.108), channel_id=1, source_target_pairs={{1,0},{0,1},{3,2},{2,3},{5,4},{4,5},{7,6},{6,7},{9,8},{8,9},{11,10... | collective-permute-start | bytes 5701640 | tf_op jit(solution)/shard_map/sum3_core/ppermute | solution.py:187
  358.2 34.6 %collective-permute-start.16 = (bf16[128,1792]{1,0:T(8,128)(2,1)S(1)}, bf16[128,1792]{1,0:T(8,128)(2,1)}, u32[]{:S(2)}, u32[]{:S(2)}) collective-permute-start(bf16[128,1792]{1,0:T(8,128)(2,1)S(1)} %slice.88), channel_id=1, source_target_pairs={{8,0},{9,1},{10,2},{11,3},{12,4},{13,5},{14,6},{15,7},{0,8},{1,9},... | collective-permute-start | bytes 1376264 | tf_op jit(solution)/shard_map/sum2_z/ppermute | solution.py:187
  361.4 67.3 %collective-permute-start.19 = (bf16[128,3712]{1,0:T(8,128)(2,1)}, bf16[128,3712]{1,0:T(8,128)(2,1)}, u32[]{:S(2)}, u32[]{:S(2)}) collective-permute-start(bf16[128,3712]{1,0:T(8,128)(2,1)} %add_convert_fusion.5), channel_id=1, source_target_pairs={{12,0},{13,1},{14,2},{15,3},{0,4},{1,5},{2,6},{3,7},{4,8},{5,9},{6... | collective-permute-start | bytes 2850824 | tf_op jit(solution)/shard_map/sum1_z/ppermute | solution.py:187
  361.9 14.8 %slice-start.2 = ((s8[9175040]{0:T(1024)(128)(4,1)}), s8[4194304]{0:T(1024)(128)(4,1)S(1)}, s32[]{:S(2)}) async-start(s8[9175040]{0:T(1024)(128)(4,1)} %bitcast.88), calls=%async_computation.4 | async-start | bytes 8388608
  363.6 26.7 %collective-permute-start.15 = (bf16[128,3712]{1,0:T(8,128)(2,1)}, bf16[128,3712]{1,0:T(8,128)(2,1)}, u32[]{:S(2)}, u32[]{:S(2)}) collective-permute-start(bf16[128,3712]{1,0:T(8,128)(2,1)} %get-tuple-element.122), channel_id=1, source_target_pairs={{2,0},{3,1},{0,2},{1,3},{6,4},{7,5},{4,6},{5,7},{10,8},{11,9},{8,1... | collective-permute-start | bytes 2850824 | tf_op jit(solution)/shard_map/sum3_y/ppermute | solution.py:187
  363.9 12.8 %slice-start.3 = ((s8[9175040]{0:T(1024)(128)(4,1)}), s8[4194304]{0:T(1024)(128)(4,1)S(1)}, s32[]{:S(2)}) async-start(s8[9175040]{0:T(1024)(128)(4,1)} %bitcast.88), calls=%async_computation.5 | async-start | bytes 8388608
  363.9 12.8 %slice-start.4 = ((s8[9175040]{0:T(1024)(128)(4,1)}), s8[786432]{0:T(1024)(128)(4,1)S(1)}, s32[]{:S(2)}) async-start(s8[9175040]{0:T(1024)(128)(4,1)} %bitcast.88), calls=%async_computation.6 | async-start | bytes 1572864
  376.7 13.6 %copy-start.15 = (bf16[128,3712]{1,0:T(8,128)(2,1)S(1)}, bf16[128,3712]{1,0:T(8,128)(2,1)}, u32[]{:S(2)}) copy-start(bf16[128,3712]{1,0:T(8,128)(2,1)} %get-tuple-element.115) | copy-start | bytes 2850820
  390.3 3.4 copy-start.14
  392.8 23.3 %collective-permute-start.17 = (bf16[2,128,3712]{2,1,0:T(8,128)(2,1)S(1)}, bf16[2,128,3712]{2,1,0:T(8,128)(2,1)S(1)}, u32[]{:S(2)}, u32[]{:S(2)}) collective-permute-start(bf16[2,128,3712]{2,1,0:T(8,128)(2,1)S(1)} %get-tuple-element.116), channel_id=1, source_target_pairs={{1,0},{0,1},{3,2},{2,3},{5,4},{4,5},{7,6},{6,7},{9,8},{8,9},{11,10... | collective-permute-start | bytes 5701640 | tf_op jit(solution)/shard_map/sum0_core/ppermute | solution.py:187
  393.7 23.0 %slice-start.5 = ((s8[9175040]{0:T(1024)(128)(4,1)}), s8[4194304]{0:T(1024)(128)(4,1)S(1)}, s32[]{:S(2)}) async-start(s8[9175040]{0:T(1024)(128)(4,1)} %bitcast.90), calls=%async_computation.7 | async-start | bytes 8388608
  393.7 23.0 %slice-start.6 = ((s8[9175040]{0:T(1024)(128)(4,1)}), s8[4194304]{0:T(1024)(128)(4,1)S(1)}, s32[]{:S(2)}) async-start(s8[9175040]{0:T(1024)(128)(4,1)} %bitcast.90), calls=%async_computation.8 | async-start | bytes 8388608
  393.7 23.0 %slice-start.7 = ((s8[9175040]{0:T(1024)(128)(4,1)}), s8[786432]{0:T(1024)(128)(4,1)S(1)}, s32[]{:S(2)}) async-start(s8[9175040]{0:T(1024)(128)(4,1)} %bitcast.90), calls=%async_computation.9 | async-start | bytes 1572864
  405.4 11.2 %copy-start.13 = (bf16[1280,1024]{1,0:T(8,128)(2,1)S(1)}, bf16[1280,1024]{1,0:T(8,128)(2,1)}, u32[]{:S(2)}) copy-start(bf16[1280,1024]{1,0:T(8,128)(2,1)} %get-tuple-element.119) | copy-start | bytes 7864324
  405.4 31.4 %collective-permute-start.20 = (bf16[128,3712]{1,0:T(8,128)(2,1)}, bf16[128,3712]{1,0:T(8,128)(2,1)S(1)}, u32[]{:S(2)}, u32[]{:S(2)}) collective-permute-start(bf16[128,3712]{1,0:T(8,128)(2,1)} %add_convert_fusion.2), channel_id=1, source_target_pairs={{4,0},{5,1},{6,2},{7,3},{8,4},{9,5},{10,6},{11,7},{12,8},{13,9},{1... | collective-permute-start | bytes 2850824 | tf_op jit(solution)/shard_map/sum3_z/ppermute | solution.py:187
  416.3 22.4 %collective-permute-start.18 = (bf16[128,3712]{1,0:T(8,128)(2,1)S(1)}, bf16[128,3712]{1,0:T(8,128)(2,1)S(1)}, u32[]{:S(2)}, u32[]{:S(2)}) collective-permute-start(bf16[128,3712]{1,0:T(8,128)(2,1)S(1)} %fusion.13), channel_id=1, source_target_pairs={{2,0},{3,1},{0,2},{1,3},{6,4},{7,5},{4,6},{5,7},{10,8},{11,9},{8,1... | collective-permute-start | bytes 2850824 | tf_op jit(solution)/shard_map/sum0_y/ppermute | solution.py:187
  416.7 22.0 %copy-start.17 = (bf16[128,1920]{1,0:T(8,128)(2,1)S(1)}, bf16[128,1920]{1,0:T(8,128)(2,1)}, u32[]{:S(2)}) copy-start(bf16[128,1920]{1,0:T(8,128)(2,1)} %copy-done.16) | copy-start | bytes 1474564
  440.7 1.1 copy-start.18
  (2 other events, 1.6 us)
Sparse Core Ops, SparseCore 0:
  11.0 115.9 all-gather.4
  129.3 112.0 all-gather.6
